TPU v7x, 256 devices: a whole 4x4x8 slice. The times are simulated.
256 devices in a mesh: lat: 16 (over x, y_hi, core), lon: 16 (over y_lo, z).
Axes of the slice: x: 4, y: 4 (y_hi: 2, y_lo: 2; y = y_hi * 2 + y_lo), z: 8, core: 2. Of those that a mesh axis runs over, the one named last changes fastest.
Arguments:
- tracer: float32 [32, 512, 2048], P(None, 'lat', 'lon'), may hold values from -6 to 6
- source: int32 [512, 16], P('lat', 'lon'), may hold values from 0 to 8191, as said below
- offset: int32 [512, 2048], P('lat', 'lon'), may hold values from 1 to 125
- fraction: float32 [512, 2048], P('lat', 'lon'), may hold values from 0 to 1
- cutoffs: int32 [2, 8], replicated, may hold values from 2 to 255
Outputs:
- advected: float32 [32, 512, 2048], P(None, 'lat', 'lon')
Inputs may be any that keep to these rules, and one draw needn't show every extreme that they name: With source[j, b] = rho * 16 + beta: |rho - j| <= 2, and some arrival blocks reach 2 in both directions. Rows j with 8 <= j < 504 have beta equal to b - 1, b or b + 1 modulo 16. Rows within 8 of a pole have rho within the same band of 8 rows at that pole and beta anywhere on the circle.
All inputs are finite; a program needn't handle non-finite values.
Results may differ from a plain program's by a relative error of at most 0.000071.
Values sent between devices are 32-bit elements; how exact they have to be, the bound alone decides.
No kernel may reach another device: no remote copies, remote signals or barrier semaphores. Data moves between devices by JAX's collectives and lax.ppermute only.
A program may use at most 128 MiB of HBM per device.

v0:
```python
import math

import jax
import jax.numpy as jnp
from jax import lax
from jax.sharding import PartitionSpec as P

NLON = 2048
BLK = 128
HL = 2
PROWS = 8


def extended(cells, sides, width, closed):
    for axis, dim in sides:
        count = lax.axis_size(axis)
        ends = count if closed else count - 1
        head = lax.slice_in_dim(cells, 0, width, axis=dim)
        tail = lax.slice_in_dim(cells, cells.shape[dim] - width, cells.shape[dim], axis=dim)
        cells = jnp.concatenate(
            [
                lax.ppermute(tail, axis, [(i, (i + 1) % count) for i in range(ends)]),
                cells,
                lax.ppermute(head, axis, [((i + 1) % count, i) for i in range(ends)]),
            ],
            axis=dim,
        )
    return cells


def cubic_limited(before_one, at_anchor, after_one, after_two, position):
    weight_before = -position * (position - 1.0) * (position - 2.0) / 6.0
    weight_anchor = (position + 1.0) * (position - 1.0) * (position - 2.0) / 2.0
    weight_after = -(position + 1.0) * position * (position - 2.0) / 2.0
    weight_beyond = (position + 1.0) * position * (position - 1.0) / 6.0
    interpolated = (
        weight_before * before_one
        + weight_anchor * at_anchor
        + weight_after * after_one
        + weight_beyond * after_two
    )
    lowest_bound = jnp.minimum(at_anchor, after_one)
    upper_bound = jnp.maximum(at_anchor, after_one)
    return jnp.minimum(jnp.maximum(interpolated, lowest_bound), upper_bound)


def spectral_table(first_cell, cell_total):
    cell_ids = first_cell + jnp.arange(cell_total, dtype=jnp.int32)
    wavenumbers = jnp.arange(NLON // 2, dtype=jnp.int32)
    phases = cell_ids[:, None] * wavenumbers[None, :] % NLON
    angles = phases.astype(jnp.float32) * (2.0 * math.pi / NLON)
    return jnp.concatenate([jnp.cos(angles), jnp.sin(angles)], axis=1)


def damping_rows(cutoff_values):
    wavenumbers = jnp.arange(NLON // 2, dtype=jnp.int32)
    ratios = cutoff_values.astype(jnp.float32)[..., None] / jnp.maximum(wavenumbers, 1).astype(
        jnp.float32
    )
    half_weights = jnp.where(wavenumbers >= 1, jnp.maximum(1.0 - ratios, 0.0), 0.0) * (2.0 / NLON)
    return jnp.concatenate([half_weights, half_weights], axis=-1)


def take_cells(values, indices):
    return jnp.take(values, indices, axis=1)


def polar_work(slab_data, source_rows, source_cells, positions, cutoff_rows, first_cell, lon_width):
    pole_count = slab_data.shape[0]
    channel_count = slab_data.shape[1]
    cell_span = PROWS * lon_width
    flat_rows = source_rows.reshape(pole_count, cell_span)
    flat_cells = source_cells.reshape(pole_count, cell_span)
    zeros_init = jnp.zeros((pole_count, channel_count, cell_span), jnp.float32)
    totals = (zeros_init, zeros_init, zeros_init, zeros_init)
    portion = lax.all_gather(slab_data, "lon", axis=3, tiled=True)
    length = portion.shape[3]
    flat_portion = portion.reshape(pole_count, channel_count, PROWS * length)
    results = []
    for step_offset, partial_sum in zip((-1, 0, 1, 2), totals):
        column = flat_cells + step_offset
        inside = (column >= 0) & (column < length)
        gather_index = flat_rows * length + jnp.clip(column, 0, length - 1)
        picked = jax.vmap(take_cells)(flat_portion, gather_index)
        results.append(jnp.where(inside[:, None, :], picked, 0.0))
    before_one, at_anchor, after_one, after_two = tuple(results)
    limited = cubic_limited(
        before_one, at_anchor, after_one, after_two, positions.reshape(pole_count, 1, cell_span)
    )
    shaped = limited.reshape(pole_count, channel_count, PROWS, lon_width)
    fourier_basis = spectral_table(first_cell, lon_width)
    spectra = jnp.einsum("pcrx,xk->pcrk", shaped, fourier_basis, precision=lax.Precision.HIGHEST)
    spectra = lax.psum(spectra, "lon")
    weights = damping_rows(cutoff_rows)
    removed = jnp.einsum(
        "pcrk,xk->pcrx", spectra * weights[:, None], fourier_basis, precision=lax.Precision.HIGHEST
    )
    return shaped - removed


def body(tracer, source, offset, fraction, cutoffs):
    channels, lat_rows, lon_cells = tracer.shape
    lat_count = lax.axis_size("lat")
    lat_place = lax.axis_index("lat")
    lon_place = lax.axis_index("lon")
    first_row = lat_place * lat_rows
    first_cell = lon_place * lon_cells
    all_rows = lat_rows * lat_count
    block_count = NLON // BLK
    cell_block = jnp.arange(lon_cells, dtype=jnp.int32) // BLK
    per_cell = jnp.take(source, cell_block, axis=1)
    source_row = per_cell // block_count
    source_block = per_cell % block_count
    padded_rows = extended(tracer, (("lat", 1),), HL, False)
    widened = extended(padded_rows, (("lon", 2),), BLK, True)
    row_total = lat_rows + 2 * HL
    width_total = lon_cells + 2 * BLK
    local_row = jnp.clip(source_row - first_row + HL, 0, row_total - 1)
    local_start = jnp.clip(
        jnp.mod(source_block * BLK - first_cell + BLK, NLON), 0, width_total - BLK
    )
    anchor = local_row * width_total + local_start + offset
    flat_field = widened.reshape(channels, row_total * width_total)

    def stencil(shift_by):
        return jnp.take(flat_field, (anchor + shift_by).reshape(-1), axis=1).reshape(
            channels, lat_rows, lon_cells
        )

    limited = cubic_limited(stencil(-1), stencil(0), stencil(1), stencil(2), fraction[None])
    slab_first = jnp.where(lat_place == 0, 0, lat_rows - PROWS).astype(jnp.int32)
    slab_global = first_row + slab_first
    pole_side = jnp.where(lat_place == 0, 0, 1).astype(jnp.int32)

    def rows_of(values):
        return lax.dynamic_slice_in_dim(values, slab_first, PROWS, 0)

    slab_rows = jnp.clip(rows_of(source_row) - slab_global, 0, PROWS - 1)
    slab_cells = rows_of(source_block * BLK + offset)
    slab_fraction = rows_of(fraction)
    slab_tracer = lax.dynamic_slice_in_dim(tracer, slab_first, PROWS, 1)
    cutoff_rows = lax.dynamic_slice_in_dim(cutoffs, pole_side, 1, 0)
    filtered = polar_work(
        slab_tracer[None],
        slab_rows[None],
        slab_cells[None],
        slab_fraction[None],
        cutoff_rows,
        first_cell,
        lon_cells,
    )
    polar_result = filtered.reshape(channels, PROWS, lon_cells)
    updated = lax.dynamic_update_slice_in_dim(limited, polar_result, slab_first, 1)
    global_rows = first_row + jnp.arange(lat_rows, dtype=jnp.int32)
    polar_mask = (global_rows < PROWS) | (global_rows >= all_rows - PROWS)
    return jnp.where(polar_mask[None, :, None], updated, limited)


def solution(mesh):
    placed = (P(None, "lat", "lon"), P("lat", "lon"), P("lat", "lon"), P("lat", "lon"), P())
    return jax.shard_map(
        body, mesh=mesh, in_specs=placed, out_specs=P(None, "lat", "lon"), check_vma=False
    )
```

profile of v0, /device:TPU:32, one launch (start us, length us, event | category | flops | bytes accessed | tf_op | source)
XLA Modules:
  0.0 309.7 jit_solution(2607581117400287599)
XLA Ops:
  6.5 1.0 fusion.89
  7.6 1.7 collective-permute-start
  9.3 1.3 collective-permute-start.1
  10.6 1.6 constant_dynamic-slice_fusion.1
  12.3 0.7 add_select_fusion.3
  13.8 0.8 compare_and_fusion.3
  15.8 1.4 constant_dynamic-update-slice_fusion.1
  17.2 1.5 collective-permute-start.3
  19.4 2.1 fusion.20
  21.5 8.8 %collective-permute-done.3 = f32[32,36,128]{2,0,1:T(8,128)S(1)} collective-permute-done((f32[32,36,128]{2,0,1:T(8,128)S(1)}, f32[32,36,128]{2,0,1:T(8,128)S(1)}, u32[]{:S(2)}, u32[]{:S(2)}) %collective-permute-start.3) | collective-permute-done | bytes 589856 | tf_op jit(solution)/shard_map/ppermute | solution.py:24
  30.3 7.2 %collective-permute-done.2 = f32[32,36,128]{2,0,1:T(8,128)S(1)} collective-permute-done((f32[32,36,128]{2,0,1:T(8,128)S(1)}, f32[32,36,128]{2,0,1:T(8,128)S(1)}, u32[]{:S(2)}, u32[]{:S(2)}) %collective-permute-start.2) | collective-permute-done | bytes 589856 | tf_op jit(solution)/shard_map/ppermute | solution.py:22
  37.7 4.5 %copy.33 = f32[32,36,384]{0,2,1:T(8,128)} copy(f32[32,36,384]{2,0,1:T(8,128)S(1)} %pad_maximum_fusion) | data formatting | bytes 3538944 | tf_op jit(solution)/shard_map/concatenate | solution.py:20
  42.2 17.2 %gather_fusion.1 = f32[4096,32]{1,0:T(8,128)} fusion(f32[32,13824]{0,1:T(8,128)} %bitcast.168, s32[4096]{0:T(1024)S(1)} %get-tuple-element.28), kind=kCustom, calls=%fused_computation.2.clone | custom fusion | bytes 1064960 | tf_op jit(solution)/shard_map/jit(_take)/gather | solution.py:126
  59.4 3.6 %broadcast_select_fusion.2 = f32[4096,32]{1,0:T(8,128)S(1)} fusion(f32[4096,32]{1,0:T(8,128)} %gather_fusion.1, pred[4096]{0:T(1024)(128)(4,1)S(1)} %get-tuple-element.31), kind=kLoop, calls=%fused_computation.19 | loop fusion | flops 131072 | bytes 1052672 | tf_op jit(solution)/shard_map/jit(_take)/select_n | solution.py:126
  63.0 1.5 copy.44
  64.5 17.2 %gather_fusion.3 = f32[4096,32]{1,0:T(8,128)} fusion(f32[32,13824]{0,1:T(8,128)} %bitcast.169, s32[4096]{0:T(1024)S(1)} %get-tuple-element.26), kind=kCustom, calls=%fused_computation.4.clone | custom fusion | bytes 1064960 | tf_op jit(solution)/shard_map/jit(_take)/gather | solution.py:126
  81.7 17.2 %gather_fusion.2 = f32[4096,32]{1,0:T(8,128)} fusion(f32[32,13824]{0,1:T(8,128)} %bitcast.170, s32[4096]{0:T(1024)S(1)} %get-tuple-element.27), kind=kCustom, calls=%fused_computation.3.clone | custom fusion | bytes 1064960 | tf_op jit(solution)/shard_map/jit(_take)/gather | solution.py:126
  98.9 6.3 %copy.38 = f32[32,8,2048]{0,2,1:T(8,128)} copy(f32[32,8,2048]{2,1,0:T(8,128)} %all-gather.3.cloned.1.call-done) | data formatting | bytes 4194304 | tf_op jit(solution)/shard_map/all_gather | solution.py:76
  105.2 10.5 %gather_fusion.7 = f32[1024,32]{1,0:T(8,128)S(1)} fusion(f32[1,32,16384]{1,2,0:T(8,128)} %bitcast.176, s32[1024]{0:T(1024)S(1)} %bitcast.174), kind=kCustom, calls=%fused_computation.7.clone | custom fusion | bytes 270336 | tf_op jit(solution)/shard_map/vmap(jit(_take))/gather | solution.py:65
  115.9 10.5 %gather_fusion.4 = f32[1024,32]{1,0:T(8,128)S(1)} fusion(f32[1,32,16384]{1,2,0:T(8,128)} %bitcast.177, s32[1024]{0:T(1024)S(1)} %bitcast.175), kind=kCustom, calls=%fused_computation.1.clone | custom fusion | bytes 270336 | tf_op jit(solution)/shard_map/vmap(jit(_take))/gather | solution.py:65
  126.6 10.5 %gather_fusion.6 = f32[1024,32]{1,0:T(8,128)S(1)} fusion(f32[1,32,16384]{1,2,0:T(8,128)} %bitcast.178, s32[1024]{0:T(1024)S(1)} %bitcast.172), kind=kCustom, calls=%fused_computation.6.clone | custom fusion | bytes 270336 | tf_op jit(solution)/shard_map/vmap(jit(_take))/gather | solution.py:65
  137.3 10.6 %gather_fusion.5 = f32[1024,32]{1,0:T(8,128)S(1)} fusion(f32[1,32,16384]{1,2,0:T(8,128)} %bitcast.179, s32[1024]{0:T(1024)S(1)} %bitcast.173), kind=kCustom, calls=%fused_computation.5.clone | custom fusion | bytes 270336 | tf_op jit(solution)/shard_map/vmap(jit(_take))/gather | solution.py:65
  148.2 3.1 %convolution_bitcast_fusion = f32[1,32,8,2048]{3,2,1,0:T(8,128)} fusion(f32[32,8,128]{2,1,0:T(8,128)S(1)} %bitcast.184, f32[128,1024]{1,0:T(8,128)S(1)} %get-tuple-element.38, f32[128,1024]{1,0:T(8,128)S(1)} %get-tuple-element.37), kind=kOutput, calls=%fused_computation.8 | convolution fusion | flops 805568512 | bytes 3276800 | tf_op jit(solution)/shard_map/pcrx,xk->pcrk/dot_general | solution.py:92
  151.3 6.4 %broadcast_select_fusion = (f32[4096,32]{1,0:T(8,128)S(1)}, f32[4096,32]{1,0:T(8,128)}) fusion(f32[4096,32]{1,0:T(8,128)} %gather_fusion.3, pred[4096]{0:T(1024)(128)(4,1)S(1)} %get-tuple-element.29, f32[4096,32]{1,0:T(8,128)} %gather_fusion.2, pred[4096]{0:T(1024)(128)(4,1)S(1)} %get-tuple-element.30), kind=kLoop, calls=%fused_computation.17 | loop fusion | flops 262144 | bytes 2105344 | tf_op jit(solution)/shard_map/jit(_take)/select_n | solution.py:126
  157.7 3.1 copy.45
  160.7 1.4 copy.46
  162.2 17.2 %gather_fusion = f32[4096,32]{1,0:T(8,128)} fusion(f32[32,13824]{0,1:T(8,128)} %bitcast.171, s32[4096]{0:T(1024)S(1)} %get-tuple-element.25), kind=kCustom, calls=%fused_computation.clone | custom fusion | bytes 1064960 | tf_op jit(solution)/shard_map/jit(_take)/gather | solution.py:126
  179.4 3.6 %broadcast_select_fusion.3 = f32[4096,32]{1,0:T(8,128)S(1)} fusion(f32[4096,32]{1,0:T(8,128)} %gather_fusion, pred[4096]{0:T(1024)(128)(4,1)S(1)} %get-tuple-element.9), kind=kLoop, calls=%fused_computation.20 | loop fusion | flops 131072 | bytes 1052672 | tf_op jit(solution)/shard_map/jit(_take)/select_n | solution.py:126
  183.0 1.5 copy.43
  184.5 2.6 maximum_minimum_fusion
  187.0 111.8 %all-reduce.2.cloned.1.call-done = f32[1,32,8,2048]{3,2,1,0:T(8,128)} async-done(((f32[1,32,8,2048]{3,2,1,0:T(8,128)}), f32[1,32,8,2048]{3,2,1,0:T(8,128)}) %all-reduce.2.cloned.1.call-update) | async-done | bytes 2097168 | tf_op jit(solution)/shard_map/psum | solution.py:93
  298.8 4.1 %fusion.9 = f32[32,32,128]{2,1,0:T(8,128)} fusion(f32[32,32,128]{2,1,0:T(8,128)} %maximum_minimum_fusion, s32[]{:T(128)S(6)} %select_n.137, f32[32,8,128]{2,1,0:T(8,128)S(1)} %bitcast.185, f32[1,32,8,2048]{3,2,1,0:T(8,128)} %all-reduce.2.cloned.1.call-done, f32[8,2048]{1,0:T(8,128)S(1)} %maximum_bitcast_fusion.3, f32[128,1024]{1,0:T(8,128)S(1)} %get-tuple-element.38, ...), kind=kOutput, calls=%fused_computation.15 | convolution fusion | flops 806158336 | bytes 3604492 | tf_op jit(solution)/shard_map/pcrk,xk->pcrx/dot_general | solution.py:95
  (49 shorter events, 3.6 us)
Async XLA Ops:
  6.5 12.8 %copy-start = (f32[32,128]{1,0:T(8,128)S(1)}, f32[32,128]{1,0:T(8,128)}, u32[]{:S(2)}) copy-start(f32[32,128]{1,0:T(8,128)} %param.12) | copy-start | bytes 49156
  6.5 92.4 %all-gather.3.cloned.1.call-start = ((), (), s32[]{:S(2)}) async-start(), calls=%async_computation.1 | async-start | bytes 2228224 | tf_op jit(solution)/shard_map/all_gather | solution.py:76
  7.6 8.2 %collective-permute-start = (f32[32,2,128]{2,0,1:T(8,128)S(1)}, f32[32,2,128]{2,0,1:T(8,128)S(1)}, u32[]{:S(2)}, u32[]{:S(2)}) collective-permute-start(f32[32,2,128]{2,0,1:T(8,128)S(1)} %copy.49), channel_id=1, source_target_pairs={{0,16},{16,32},{32,48},{48,64},{64,80},{80,96},{96,112},{112,128},... | collective-permute-start | bytes 98312 | tf_op jit(solution)/shard_map/ppermute | solution.py:22
  9.3 7.8 %collective-permute-start.1 = (f32[32,2,128]{2,0,1:T(8,128)S(1)}, f32[32,2,128]{2,0,1:T(8,128)S(1)}, u32[]{:S(2)}, u32[]{:S(2)}) collective-permute-start(f32[32,2,128]{2,0,1:T(8,128)S(1)} %copy.50), channel_id=1, source_target_pairs={{16,0},{32,16},{48,32},{64,48},{80,64},{96,80},{112,96},{128,112},... | collective-permute-start | bytes 98312 | tf_op jit(solution)/shard_map/ppermute | solution.py:24
  12.2 286.6 %all-reduce.2.cloned.1.call-start = ((), (), s32[]{:S(2)}) async-start(), calls=%async_computation | async-start | bytes 4194304 | tf_op jit(solution)/shard_map/psum | solution.py:93
  17.2 13.1 %collective-permute-start.3 = (f32[32,36,128]{2,0,1:T(8,128)S(1)}, f32[32,36,128]{2,0,1:T(8,128)S(1)}, u32[]{:S(2)}, u32[]{:S(2)}) collective-permute-start(f32[32,36,128]{2,0,1:T(8,128)S(1)} %constant_dynamic-update-slice_fusion), channel_id=1, source_target_pairs={{1,0},{2,1},{3,2},{4,3},{5,4},{6,5},{7,6},{8,7},{9,8},{10,9},{11,1... | collective-permute-start | bytes 1769480 | tf_op jit(solution)/shard_map/ppermute | solution.py:24
  18.7 18.9 %collective-permute-start.2 = (f32[32,36,128]{2,0,1:T(8,128)S(1)}, f32[32,36,128]{2,0,1:T(8,128)S(1)}, u32[]{:S(2)}, u32[]{:S(2)}) collective-permute-start(f32[32,36,128]{2,0,1:T(8,128)S(1)} %constant_dynamic-update-slice_fusion), channel_id=1, source_target_pairs={{0,1},{1,2},{2,3},{3,4},{4,5},{5,6},{6,7},{7,8},{8,9},{9,10},{10,1... | collective-permute-start | bytes 1769480 | tf_op jit(solution)/shard_map/ppermute | solution.py:22
Sparse Core Ops, SparseCore 0:
  12.3 80.2 all-gather.2
  151.5 147.3 all-reduce.1
where the time goes:
time: 312 us; the launch traced here: 310 us
  local copies, waits for them, and re-layouts  134 us (43%)
  waiting for transfers between devices  128 us (41%)
  other arithmetic  21.9 us (7%)
  between operations  13.7 us (4%)
  matrix products  7.18 us (2%)
  starting transfers between devices  5.18 us (2%)
    psum x1, waiting for transfers between devices, polar_work(): spectra = lax.psum(spectra, 'lon')  112 us
    gather x4, local copies, waits for them, and re-layouts, stencil(): jnp.take(flat_field, (anchor + shift_by).reshape(-1), axis=1)  68.9 us
    gather x12, local copies, waits for them, and re-layouts, take_cells(): return jnp.take(values, indices, axis=1)  42.8 us
    select_n x3, other arithmetic, stencil(): jnp.take(flat_field, (anchor + shift_by).reshape(-1), axis=1)  13.6 us
    ppermute x2, waiting for transfers between devices, extended(): lax.ppermute(head, axis, [((i + 1) % count, i) for i in range(ends)])  8.78 us
    reshape x4, local copies, waits for them, and re-layouts, stencil(): jnp.take(flat_field, (anchor + shift_by).reshape(-1), axis=1)  7.41 us
    ppermute x2, waiting for transfers between devices, extended(): lax.ppermute(tail, axis, [(i, (i + 1) % count) for i in range(ends)])  7.24 us
    all_gather x1, local copies, waits for them, and re-layouts, polar_work(): portion = lax.all_gather(slab_data, 'lon', axis=3, tiled=True)  6.27 us
  transfers between devices with their start and end apart: 6, of which 3 were waited for; matrix products, arithmetic and copies ran while one was open for 34% of the time, Pallas kernels for 0%

commit v1 on v0

v1 whole, which is shorter than its diff:
```python
import math

import jax
import jax.numpy as jnp
import ml_dtypes
import numpy as np
from jax import lax
from jax.experimental import pallas as pl
from jax.experimental.pallas import tpu as pltpu
from jax.sharding import PartitionSpec as P

NLON = 2048
BLK = 128
NBLK = NLON // BLK
HL = 2
PROWS = 8
PADDED = 40
F32 = jnp.float32
BF16 = jnp.bfloat16


def cubic_weights(position):
    return (
        -position * (position - 1.0) * (position - 2.0) / 6.0,
        (position + 1.0) * (position - 1.0) * (position - 2.0) / 2.0,
        -(position + 1.0) * position * (position - 2.0) / 2.0,
        (position + 1.0) * position * (position - 1.0) / 6.0,
    )


def cubic_limited(values, cells, weights):
    def at(shift):
        return jnp.take_along_axis(values, cells + shift, axis=1, mode="promise_in_bounds")

    before_one, at_anchor, after_one, after_two = at(-1), at(0), at(1), at(2)
    interpolated = (
        weights[0] * before_one
        + weights[1] * at_anchor
        + weights[2] * after_one
        + weights[3] * after_two
    )
    lowest_bound = jnp.minimum(at_anchor, after_one)
    upper_bound = jnp.maximum(at_anchor, after_one)
    return jnp.minimum(jnp.maximum(interpolated, lowest_bound), upper_bound)


def two_pieces(table):
    high = table.astype(ml_dtypes.bfloat16)
    return high, (table - high.astype(np.float64)).astype(ml_dtypes.bfloat16)


def fourier_tables():
    b = np.arange(NBLK)
    angles = 2.0 * math.pi * np.outer(b, b) / NBLK
    rows = np.eye(PROWS)
    blocks = np.concatenate([np.kron(np.cos(angles), rows), -np.kron(np.sin(angles), rows)], 0)
    i = np.arange(BLK)
    angles = 2.0 * math.pi * (np.outer(i, i) % BLK) / BLK
    cosine, sine = np.cos(angles), np.sin(angles)
    cells = np.block([[cosine, -sine], [sine, cosine]])
    angles = 2.0 * math.pi * np.repeat(np.outer(b, i), PROWS, 0) / NLON
    turn = np.stack([np.cos(angles), -np.sin(angles)]).astype(np.float32)
    return (*two_pieces(blocks), *two_pieces(blocks.T.copy()), *two_pieces(cells), turn)


def dot(left, right):
    return jnp.dot(left, right, preferred_element_type=F32)


def split(values):
    high = values.astype(BF16)
    return high, (values - high.astype(F32)).astype(BF16)


def pack_kernel(first_ref, tracer, source, offset, fraction, out):
    first = pl.multiple_of(first_ref[0], PROWS)
    rows = pl.ds(first, PROWS)
    anchor = source[rows, :] * BLK + offset[rows, :]
    channels = tracer.shape[0]
    out[:, 0:2] = tracer[:, rows, :].reshape(NBLK, channels // NBLK, PROWS, BLK)
    shape = (NBLK, PROWS, BLK)
    out[:, 2] = jnp.broadcast_to(anchor.astype(F32), shape)
    out[:, 3] = jnp.broadcast_to(fraction[rows, :], shape)


def polar_kernel(
    band, weights, blocks_h, blocks_l, back_h, back_l, cells_h, cells_l, turn, out
):
    count = NBLK * PROWS
    anchor = band[:, 2].reshape(count, BLK).astype(jnp.int32)
    place = ((anchor >> 7) & 15) * PROWS + ((anchor >> 11) & 7)
    lanes = lax.broadcasted_iota(jnp.int32, (count, BLK), 1)
    chosen = jnp.where(place == lanes, 1.0, 0.0).astype(BF16)
    own = jnp.concatenate([band[:, 0].reshape(count, BLK), band[:, 1].reshape(count, BLK)], 1)
    high = own.astype(BF16)
    rest = own - high.astype(F32)
    middle = rest.astype(BF16)
    low = (rest - middle.astype(F32)).astype(BF16)
    picked = dot(chosen, high) + dot(chosen, middle) + dot(chosen, low)
    cell = anchor & 127
    cubic = cubic_weights(band[:, 3].reshape(count, BLK))
    limited = [
        cubic_limited(picked[:, :BLK], cell, cubic),
        cubic_limited(picked[:, BLK:], cell, cubic),
    ]
    turn_r, turn_i = turn[0], turn[1]
    high, low = split(jnp.concatenate(limited, 1))
    first = dot(blocks_h[...], high) + dot(blocks_h[...], low) + dot(blocks_l[...], high)
    parts = []
    for c in range(2):
        real, imag = first[:count, c * BLK : (c + 1) * BLK], first[count:, c * BLK : (c + 1) * BLK]
        parts.append(
            jnp.concatenate([real * turn_r - imag * turn_i, real * turn_i + imag * turn_r], 1)
        )
    high, low = split(jnp.concatenate(parts, 0))
    spectrum = dot(high, cells_h[...]) + dot(low, cells_h[...]) + dot(high, cells_l[...])
    damping = jnp.concatenate([weights[...], weights[...]], 0)
    damped = jnp.concatenate([spectrum[:, BLK:] * damping, spectrum[:, :BLK] * damping], 1)
    high, low = split(damped)
    second = dot(high, cells_h[...]) + dot(low, cells_h[...]) + dot(high, cells_l[...])
    reals, imags = [], []
    for c in range(2):
        imag, real = second[c * count : (c + 1) * count, :BLK], second[c * count : (c + 1) * count, BLK:]
        reals.append(real * turn_r + imag * turn_i)
        imags.append(imag * turn_r - real * turn_i)
    high, low = split(
        jnp.concatenate([jnp.concatenate(reals, 1), jnp.concatenate(imags, 1)], 0)
    )
    removed = dot(back_h[...], high) + dot(back_h[...], low) + dot(back_l[...], high)
    for c in range(2):
        kept = limited[c] - removed[:, c * BLK : (c + 1) * BLK]
        out[:, c] = kept.reshape(NBLK, PROWS, BLK)


def rows_kernel(
    place, offset, fraction, own, west, east, halo, halo_west, halo_east, out, field, cubic, sems
):
    channels, rows = own.shape[0], own.shape[1]
    span = channels * PADDED
    columns = field.reshape(3, channels, PADDED, BLK)
    copies = [
        pltpu.make_async_copy(part, columns.at[n, :, pl.ds(0, rows), :], sems.at[n])
        for n, part in enumerate((west, own, east))
    ]
    for copy in copies:
        copy.start()
    for n, part in enumerate((halo_west, halo, halo_east)):
        columns[n, :, rows : rows + 2 * HL, :] = part[...]
    for n, weight in enumerate(cubic_weights(fraction[...])):
        cubic[n] = weight
    for copy in copies:
        copy.wait()
    flat_out = out.reshape(channels * rows, BLK)
    for j in range(rows):
        values = field[pl.ds(place[j], channels, stride=PADDED), :]
        cells = jnp.broadcast_to(offset[j : j + 1, :], (channels, BLK))
        weights = [cubic[n, j : j + 1, :] for n in range(4)]
        flat_out[pl.ds(j, channels, stride=rows), :] = cubic_limited(values, cells, weights)


def merge_kernel(first_ref, polar_ref, rows_done, polar, out, sem):
    @pl.when(polar_ref[0] == 1)
    def _():
        first = pl.multiple_of(first_ref[0], PROWS)
        copy = pltpu.make_async_copy(polar, out.at[:, pl.ds(first, PROWS), :], sem)
        copy.start()
        copy.wait()


def body(tracer, source, offset, fraction, cutoffs):
    channels, rows, cells = tracer.shape
    lat_count = lax.axis_size("lat")
    lat, lon = lax.axis_index("lat"), lax.axis_index("lon")
    first_row = lat * rows
    slab = jnp.where(lat == 0, 0, rows - PROWS).astype(jnp.int32).reshape(1)
    is_polar = ((lat == 0) | (lat == lat_count - 1)).astype(jnp.int32).reshape(1)

    smem = pl.BlockSpec(memory_space=pltpu.SMEM)
    vmem = pl.BlockSpec(memory_space=pltpu.VMEM)
    anyplace = pl.BlockSpec(memory_space=pl.ANY)

    with jax.named_scope("pack_polar_band"):
        packed = pl.pallas_call(
            pack_kernel,
            out_shape=jax.ShapeDtypeStruct((NBLK, 4, PROWS, BLK), F32),
            in_specs=[smem, vmem, vmem, vmem, vmem],
            out_specs=vmem,
            compiler_params=pltpu.CompilerParams(vmem_limit_bytes=8 << 20),
            cost_estimate=pl.CostEstimate(flops=0, bytes_accessed=1 << 20, transcendentals=0),
        )(slab, tracer, source, offset, fraction)

    with jax.named_scope("halos"):
        up = [(n, n + 1) for n in range(lat_count - 1)]
        down = [(n + 1, n) for n in range(lat_count - 1)]
        around = [(n, (n + 1) % NBLK) for n in range(NBLK)]
        back = [((n + 1) % NBLK, n) for n in range(NBLK)]
        west = lax.ppermute(tracer, "lon", around)
        east = lax.ppermute(tracer, "lon", back)
        north = lax.ppermute(tracer[:, rows - HL :, :], "lat", up)
        south = lax.ppermute(tracer[:, :HL, :], "lat", down)
        halo = jnp.concatenate([north, south], 1)
        halo_west = lax.ppermute(halo, "lon", around)
        halo_east = lax.ppermute(halo, "lon", back)

    with jax.named_scope("polar_rows"):
        band = lax.all_to_all(packed, "lon", 0, 0)
        kappa = jnp.where(lat == 0, cutoffs[0], cutoffs[1]).astype(F32)
        k1 = jnp.arange(NBLK, dtype=jnp.int32)
        k2 = jnp.arange(BLK, dtype=jnp.int32)
        wave = k1[:, None, None] + NBLK * k2[None, None, :]
        wave = jnp.minimum(wave, NLON - wave)
        inside = (wave >= 1) & (wave < NLON // 2)
        ratio = kappa[None, :, None] / jnp.maximum(wave, 1).astype(F32)
        damping = jnp.where(inside, jnp.maximum(1.0 - ratio, 0.0), 0.0) * (1.0 / NLON)
        filtered = pl.pallas_call(
            polar_kernel,
            out_shape=jax.ShapeDtypeStruct((NBLK, 2, PROWS, BLK), F32),
            in_specs=[vmem] * 9,
            out_specs=vmem,
            compiler_params=pltpu.CompilerParams(vmem_limit_bytes=16 << 20),
            cost_estimate=pl.CostEstimate(
                flops=400_000_000, bytes_accessed=2 << 20, transcendentals=0
            ),
        )(band, damping.reshape(NBLK * PROWS, BLK), *fourier_tables())
        polar = lax.all_to_all(filtered, "lon", 0, 0).reshape(channels, PROWS, BLK)

    with jax.named_scope("other_rows"):
        row = source[:, 0] // NBLK - first_row
        row = jnp.where(row < 0, row + rows + HL, jnp.where(row >= rows, row + HL, row))
        row = jnp.clip(row, 0, rows + 2 * HL - 1)
        column = jnp.clip(jnp.mod(source[:, 0] % NBLK - lon + 1, NBLK), 0, 2)
        place = column * (channels * PADDED) + row
        done = pl.pallas_call(
            rows_kernel,
            out_shape=jax.ShapeDtypeStruct(tracer.shape, F32),
            in_specs=[smem, vmem, vmem, anyplace, anyplace, anyplace, vmem, vmem, vmem],
            out_specs=vmem,
            scratch_shapes=[
                pltpu.VMEM((3 * channels * PADDED, BLK), F32),
                pltpu.VMEM((4, rows, BLK), F32),
                pltpu.SemaphoreType.DMA((3,)),
            ],
            compiler_params=pltpu.CompilerParams(vmem_limit_bytes=16 << 20),
            cost_estimate=pl.CostEstimate(
                flops=4_000_000, bytes_accessed=8 << 20, transcendentals=0
            ),
        )(place, offset, fraction, tracer, west, east, halo, halo_west, halo_east)

    with jax.named_scope("merge"):
        return pl.pallas_call(
            merge_kernel,
            out_shape=jax.ShapeDtypeStruct(tracer.shape, F32),
            in_specs=[smem, smem, anyplace, anyplace],
            out_specs=anyplace,
            scratch_shapes=[pltpu.SemaphoreType.DMA],
            input_output_aliases={2: 0},
            compiler_params=pltpu.CompilerParams(vmem_limit_bytes=4 << 20),
        )(slab, is_polar, done, polar)


def solution(mesh):
    placed = (P(None, "lat", "lon"), P("lat", "lon"), P("lat", "lon"), P("lat", "lon"), P())
    return jax.shard_map(
        body, mesh=mesh, in_specs=placed, out_specs=P(None, "lat", "lon"), check_vma=False
    )
```

time: 312 us -> 50.4 us (0.16)
  the two profiles are of different devices: /device:TPU:32 before, /device:TPU:4 now
where the time goes in v1:
time: 50.4 us; the launch traced here: 50 us
  starting transfers between devices  29.3 us (58%)
  waiting for transfers between devices  12.1 us (24%)
  Pallas kernels  5.89 us (12%)
  local copies, waits for them, and re-layouts  2.28 us (5%)
    all_to_all x1, waiting for transfers between devices, body(): band = lax.all_to_all(packed, 'lon', 0, 0)  8.81 us
    all_to_all x1, starting transfers between devices, body(): band = lax.all_to_all(packed, 'lon', 0, 0)  6.09 us
    ppermute x1, starting transfers between devices, body(): south = lax.ppermute(tracer[:, :HL, :], 'lat', down)  6.05 us
    ppermute x1, starting transfers between devices, body(): east = lax.ppermute(tracer, 'lon', back)  4.95 us
    all_to_all x1, starting transfers between devices, body(): polar = lax.all_to_all(filtered, 'lon', 0, 0).reshape(channels, PROWS, BLK)  4.15 us
    ppermute x1, waiting for transfers between devices, body(): halo_west = lax.ppermute(halo, 'lon', around)  3.23 us
    pallas_call x1, Pallas kernels, body(): pl.pallas_call(rows_kernel, out_shape=jax.ShapeDtypeStruct(tracer.shape,...  2.7 us
    pallas_call x1, Pallas kernels, body(): pl.pallas_call(polar_kernel, out_shape=jax.ShapeDtypeStruct((NBLK, 2, PRO...  2.39 us
  transfers between devices with their start and end apart: 8, of which 2 were waited for; matrix products, arithmetic and copies ran while one was open for 3% of the time, Pallas kernels for 12%

profile of v1, /device:TPU:4, one launch (start us, length us, event | category | flops | bytes accessed | tf_op | source)
XLA Modules:
  0.0 50.0 jit_solution(4329316562536111448)
XLA Ops:
  0.0 1.9 %collective-permute-start = (f32[32,32,128]{2,1,0:T(8,128)}, f32[32,32,128]{2,1,0:T(8,128)S(1)}, u32[]{:S(2)}, u32[]{:S(2)}) collective-permute-start(f32[32,32,128]{2,1,0:T(8,128)} %tracer.1), channel_id=1, source_target_pairs={{0,1},{1,2},{2,3},{3,4},{4,5},{5,6},{6,7},{7,8},{8,9},{9,10},{10,1... | collective-permute-start | bytes 1572872 | tf_op jit(solution)/shard_map/halos/ppermute | solution.py:197
  1.9 5.0 %collective-permute-start.1 = (f32[32,32,128]{2,1,0:T(8,128)}, f32[32,32,128]{2,1,0:T(8,128)S(1)}, u32[]{:S(2)}, u32[]{:S(2)}) collective-permute-start(f32[32,32,128]{2,1,0:T(8,128)} %tracer.1), channel_id=1, source_target_pairs={{1,0},{2,1},{3,2},{4,3},{5,4},{6,5},{7,6},{8,7},{9,8},{10,9},{11,1... | collective-permute-start | bytes 1572872 | tf_op jit(solution)/shard_map/halos/ppermute | solution.py:198
  6.9 1.0 %fusion.15 = (f32[32,2,128]{2,1,0:T(2,128)S(1)}, f32[32,2,128]{2,1,0:T(2,128)S(1)}) fusion(f32[32,32,128]{2,1,0:T(8,128)} %tracer.1), kind=kLoop, calls=%fused_computation.32 | loop fusion | bytes 131072 | tf_op jit(solution)/shard_map/halos/slice | solution.py:199
  7.9 0.0 copy-start.3
  7.9 0.0 copy-start.2
  7.9 1.9 %collective-permute-start.2 = (f32[32,2,128]{2,1,0:T(2,128)S(1)}, f32[32,2,128]{2,1,0:T(2,128)S(1)}, u32[]{:S(2)}, u32[]{:S(2)}) collective-permute-start(f32[32,2,128]{2,1,0:T(2,128)S(1)} %get-tuple-element.5), channel_id=1, source_target_pairs={{0,16},{16,32},{32,48},{48,64},{64,80},{80,96},{96,112},{112,128},... | collective-permute-start | bytes 98312 | tf_op jit(solution)/shard_map/halos/ppermute | solution.py:199
  9.8 6.0 %collective-permute-start.3 = (f32[32,2,128]{2,1,0:T(2,128)S(1)}, f32[32,2,128]{2,1,0:T(2,128)S(1)}, u32[]{:S(2)}, u32[]{:S(2)}) collective-permute-start(f32[32,2,128]{2,1,0:T(2,128)S(1)} %get-tuple-element.6), channel_id=1, source_target_pairs={{16,0},{32,16},{48,32},{64,48},{80,64},{96,80},{112,96},{128,112},... | collective-permute-start | bytes 98312 | tf_op jit(solution)/shard_map/halos/ppermute | solution.py:200
  15.9 0.0 copy-done.11
  15.9 0.1 copy.15.source
  16.0 0.0 copy-done.2
  16.0 1.0 %copy-done = f32[32,32,128]{2,1,0:T(8,128)S(1)} copy-done((f32[32,32,128]{2,1,0:T(8,128)S(1)}, f32[32,32,128]{2,1,0:T(8,128)}, u32[]{:S(2)}) %copy-start) | copy-done | bytes 524312
  17.0 0.8 %pack_polar_band.1 = f32[16,4,8,128]{3,2,1,0:T(8,128)} custom-call(s32[1]{0:T(128)} %bitcast.first_ref, f32[32,32,128]{2,1,0:T(8,128)S(1)} %copy-done, s32[32,1]{1,0:T(8,128)S(1)} %copy.15.source, s32[32,128]{1,0:T(8,128)S(1)} %copy-done.2, f32[32,128]{1,0:T(8,128)S(1)} %copy-done.3), custom_call_target="tpu_custom_call" | custom-call | bytes 1048576 | tf_op jit(solution)/shard_map/pack_polar_band/pallas_call | solution.py:183
  17.8 0.0 copy-start.8
  17.8 0.0 copy-start.9
  17.9 6.1 %all-to-all-start = ((f32[16,4,8,128]{3,2,1,0:T(8,128)}), f32[16,4,8,128]{3,2,1,0:T(8,128)S(1)}, u32[]{:S(2)}, u32[]{:S(2)}) async-start(f32[16,4,8,128]{3,2,1,0:T(8,128)} %pack_polar_band.1), calls=%async_computation | async-start | bytes 524288 | tf_op jit(solution)/shard_map/polar_rows/all_to_all | solution.py:206
  24.0 0.0 copy-start.7
  24.0 0.1 div.37
  24.1 0.1 fusion.3.weights
  24.2 8.8 %all-to-all-done.band = f32[16,4,8,128]{3,2,1,0:T(8,128)S(1)} async-done(((f32[16,4,8,128]{3,2,1,0:T(8,128)}), f32[16,4,8,128]{3,2,1,0:T(8,128)S(1)}, u32[]{:S(2)}, u32[]{:S(2)}) %all-to-all-start) | async-done | bytes 262176 | tf_op jit(solution)/shard_map/polar_rows/all_to_all | solution.py:206
  33.1 0.0 copy-start.1
  33.1 2.4 %polar_rows.1 = f32[16,2,8,128]{3,2,1,0:T(8,128)} custom-call(f32[16,4,8,128]{3,2,1,0:T(8,128)S(1)} %all-to-all-done.band, f32[128,128]{1,0:T(8,128)S(1)} %fusion.3.weights, bf16[256,128]{1,0:T(8,128)(2,1)S(1)} %copy-done.7, bf16[256,128]{1,0:T(8,128)(2,1)S(1)} %copy-done.8, bf16[128,256]{1,0:T(8,128)(2,1)S(1)} %copy-done.9, ...), custom_call_target="tpu_custom_call" | custom-call | flops 400000000 | bytes 2097152 | tf_op jit(solution)/shard_map/polar_rows/pallas_call | solution.py:215
  35.5 4.2 %all-to-all-start.1 = ((f32[16,2,8,128]{3,2,1,0:T(8,128)}), f32[16,2,8,128]{3,2,1,0:T(8,128)S(1)}, u32[]{:S(2)}, u32[]{:S(2)}) async-start(f32[16,2,8,128]{3,2,1,0:T(8,128)} %polar_rows.1), calls=%async_computation.1 | async-start | bytes 262144 | tf_op jit(solution)/shard_map/polar_rows/all_to_all | solution.py:225
  39.7 0.0 collective-permute-done.2
  39.7 0.0 collective-permute-done.3
  39.7 2.0 %collective-permute-start.4 = (f32[32,4,128]{2,1,0:T(4,128)S(1)}, f32[32,4,128]{2,1,0:T(4,128)S(1)}, u32[]{:S(2)}, u32[]{:S(2)}) collective-permute-start(f32[32,4,128]{2,1,0:T(4,128)S(1)} %pad_maximum_fusion.halo), channel_id=1, source_target_pairs={{0,1},{1,2},{2,3},{3,4},{4,5},{5,6},{6,7},{7,8},{8,9},{9,10},{10,1... | collective-permute-start | bytes 196616 | tf_op jit(solution)/shard_map/halos/ppermute | solution.py:202
  41.7 2.2 %collective-permute-start.5 = (f32[32,4,128]{2,1,0:T(4,128)S(1)}, f32[32,4,128]{2,1,0:T(4,128)S(1)}, u32[]{:S(2)}, u32[]{:S(2)}) collective-permute-start(f32[32,4,128]{2,1,0:T(4,128)S(1)} %pad_maximum_fusion.halo), channel_id=1, source_target_pairs={{1,0},{2,1},{3,2},{4,3},{5,4},{6,5},{7,6},{8,7},{9,8},{10,9},{11,1... | collective-permute-start | bytes 196616 | tf_op jit(solution)/shard_map/halos/ppermute | solution.py:203
  44.0 3.2 %collective-permute-done.4.halo_west = f32[32,4,128]{2,1,0:T(4,128)S(1)} collective-permute-done((f32[32,4,128]{2,1,0:T(4,128)S(1)}, f32[32,4,128]{2,1,0:T(4,128)S(1)}, u32[]{:S(2)}, u32[]{:S(2)}) %collective-permute-start.4) | collective-permute-done | bytes 65568 | tf_op jit(solution)/shard_map/halos/ppermute | solution.py:202
  47.2 0.0 collective-permute-done.5.halo_east
  47.2 0.0 collective-permute-done.west
  47.2 0.0 collective-permute-done.1.east
  47.2 2.7 %other_rows.1.rows_done = f32[32,32,128]{2,1,0:T(8,128)} custom-call(s32[32]{0:T(128)S(1)} %fusion.13.place, s32[32,128]{1,0:T(8,128)S(1)} %copy-done.2, f32[32,128]{1,0:T(8,128)S(1)} %copy-done.3, f32[32,32,128]{2,1,0:T(8,128)S(1)} %copy-done.1, f32[32,32,128]{2,1,0:T(8,128)S(1)} %collective-permute-done.west, ...), custom_call_target="tpu_custom_call" | custom-call | flops 4000000 | bytes 8388608 | tf_op jit(solution)/shard_map/other_rows/pallas_call | solution.py:233
  49.9 0.0 all-to-all-done.1
  (25 shorter events, 0.1 us)
Async XLA Ops:
  0.0 47.2 %collective-permute-start = (f32[32,32,128]{2,1,0:T(8,128)}, f32[32,32,128]{2,1,0:T(8,128)S(1)}, u32[]{:S(2)}, u32[]{:S(2)}) collective-permute-start(f32[32,32,128]{2,1,0:T(8,128)} %tracer.1), channel_id=1, source_target_pairs={{0,1},{1,2},{2,3},{3,4},{4,5},{5,6},{6,7},{7,8},{8,9},{9,10},{10,1... | collective-permute-start | bytes 1572872 | tf_op jit(solution)/shard_map/halos/ppermute | solution.py:197
  1.9 45.3 %collective-permute-start.1 = (f32[32,32,128]{2,1,0:T(8,128)}, f32[32,32,128]{2,1,0:T(8,128)S(1)}, u32[]{:S(2)}, u32[]{:S(2)}) collective-permute-start(f32[32,32,128]{2,1,0:T(8,128)} %tracer.1), channel_id=1, source_target_pairs={{1,0},{2,1},{3,2},{4,3},{5,4},{6,5},{7,6},{8,7},{9,8},{10,9},{11,1... | collective-permute-start | bytes 1572872 | tf_op jit(solution)/shard_map/halos/ppermute | solution.py:198
  6.9 9.0 %copy-start.11 = (s32[32,1]{0,1:T(1,128)S(1)}, s32[32,1]{0,1:T(1,128)}, u32[]{:S(2)}) copy-start(s32[32,1]{0,1:T(1,128)} %param.13) | copy-start | bytes 388
  7.9 8.1 %copy-start.3 = (f32[32,128]{1,0:T(8,128)S(1)}, f32[32,128]{1,0:T(8,128)}, u32[]{:S(2)}) copy-start(f32[32,128]{1,0:T(8,128)} %fraction.3) | copy-start | bytes 49156
  7.9 8.1 %copy-start.2 = (s32[32,128]{1,0:T(8,128)S(1)}, s32[32,128]{1,0:T(8,128)}, u32[]{:S(2)}) copy-start(s32[32,128]{1,0:T(8,128)} %offset.3) | copy-start | bytes 49156
  7.9 31.8 %collective-permute-start.2 = (f32[32,2,128]{2,1,0:T(2,128)S(1)}, f32[32,2,128]{2,1,0:T(2,128)S(1)}, u32[]{:S(2)}, u32[]{:S(2)}) collective-permute-start(f32[32,2,128]{2,1,0:T(2,128)S(1)} %get-tuple-element.5), channel_id=1, source_target_pairs={{0,16},{16,32},{32,48},{48,64},{64,80},{80,96},{96,112},{112,128},... | collective-permute-start | bytes 98312 | tf_op jit(solution)/shard_map/halos/ppermute | solution.py:199
  9.8 29.8 %collective-permute-start.3 = (f32[32,2,128]{2,1,0:T(2,128)S(1)}, f32[32,2,128]{2,1,0:T(2,128)S(1)}, u32[]{:S(2)}, u32[]{:S(2)}) collective-permute-start(f32[32,2,128]{2,1,0:T(2,128)S(1)} %get-tuple-element.6), channel_id=1, source_target_pairs={{16,0},{32,16},{48,32},{64,48},{80,64},{96,80},{112,96},{128,112},... | collective-permute-start | bytes 98312 | tf_op jit(solution)/shard_map/halos/ppermute | solution.py:200
  16.0 1.0 %copy-start = (f32[32,32,128]{2,1,0:T(8,128)S(1)}, f32[32,32,128]{2,1,0:T(8,128)}, u32[]{:S(2)}) copy-start(f32[32,32,128]{2,1,0:T(8,128)} %tracer.1) | copy-start | bytes 1572868
  17.0 16.0 %copy-start.10 = (bf16[128,256]{1,0:T(8,128)(2,1)S(1)}, bf16[128,256]{1,0:T(8,128)(2,1)}, u32[]{:S(2)}) copy-start(bf16[128,256]{1,0:T(8,128)(2,1)} %constant.88.clone.back_l) | copy-start | bytes 196612
  17.8 6.2 %copy-start.12 = (s32[2,8]{1,0:T(2,128)S(1)}, s32[2,8]{1,0:T(2,128)}, u32[]{:S(2)}) copy-start(s32[2,8]{1,0:T(2,128)} %param.16) | copy-start | bytes 196
  17.8 15.2 %copy-start.4 = (bf16[256,256]{1,0:T(8,128)(2,1)S(1)}, bf16[256,256]{1,0:T(8,128)(2,1)}, u32[]{:S(2)}) copy-start(bf16[256,256]{1,0:T(8,128)(2,1)} %constant.89.clone.cells_h) | copy-start | bytes 393220
  17.8 15.2 %copy-start.5 = (bf16[256,256]{1,0:T(8,128)(2,1)S(1)}, bf16[256,256]{1,0:T(8,128)(2,1)}, u32[]{:S(2)}) copy-start(bf16[256,256]{1,0:T(8,128)(2,1)} %constant.90.clone.cells_l) | copy-start | bytes 393220
  17.8 15.2 %copy-start.6 = (f32[2,128,128]{2,1,0:T(8,128)S(1)}, f32[2,128,128]{2,1,0:T(8,128)}, u32[]{:S(2)}) copy-start(f32[2,128,128]{2,1,0:T(8,128)} %constant.91.clone.turn) | copy-start | bytes 393220
  17.8 15.2 %copy-start.8 = (bf16[256,128]{1,0:T(8,128)(2,1)S(1)}, bf16[256,128]{1,0:T(8,128)(2,1)}, u32[]{:S(2)}) copy-start(bf16[256,128]{1,0:T(8,128)(2,1)} %constant.86.clone.blocks_l) | copy-start | bytes 196612
  17.8 15.2 %copy-start.9 = (bf16[128,256]{1,0:T(8,128)(2,1)S(1)}, bf16[128,256]{1,0:T(8,128)(2,1)}, u32[]{:S(2)}) copy-start(bf16[128,256]{1,0:T(8,128)(2,1)} %constant.87.clone.back_h) | copy-start | bytes 196612
  17.9 15.2 %all-to-all-start = ((f32[16,4,8,128]{3,2,1,0:T(8,128)}), f32[16,4,8,128]{3,2,1,0:T(8,128)S(1)}, u32[]{:S(2)}, u32[]{:S(2)}) async-start(f32[16,4,8,128]{3,2,1,0:T(8,128)} %pack_polar_band.1), calls=%async_computation | async-start | bytes 524288 | tf_op jit(solution)/shard_map/polar_rows/all_to_all | solution.py:206
  24.0 9.1 %copy-start.7 = (bf16[256,128]{1,0:T(8,128)(2,1)S(1)}, bf16[256,128]{1,0:T(8,128)(2,1)}, u32[]{:S(2)}) copy-start(bf16[256,128]{1,0:T(8,128)(2,1)} %constant.85.clone.blocks_h) | copy-start | bytes 196612
  33.1 14.1 %copy-start.1 = (f32[32,32,128]{2,1,0:T(8,128)S(1)}, f32[32,32,128]{2,1,0:T(8,128)}, u32[]{:S(2)}) copy-start(f32[32,32,128]{2,1,0:T(8,128)} %tracer.1) | copy-start | bytes 1572868
  35.5 14.4 %all-to-all-start.1 = ((f32[16,2,8,128]{3,2,1,0:T(8,128)}), f32[16,2,8,128]{3,2,1,0:T(8,128)S(1)}, u32[]{:S(2)}, u32[]{:S(2)}) async-start(f32[16,2,8,128]{3,2,1,0:T(8,128)} %polar_rows.1), calls=%async_computation.1 | async-start | bytes 262144 | tf_op jit(solution)/shard_map/polar_rows/all_to_all | solution.py:225
  39.7 7.5 %collective-permute-start.4 = (f32[32,4,128]{2,1,0:T(4,128)S(1)}, f32[32,4,128]{2,1,0:T(4,128)S(1)}, u32[]{:S(2)}, u32[]{:S(2)}) collective-permute-start(f32[32,4,128]{2,1,0:T(4,128)S(1)} %pad_maximum_fusion.halo), channel_id=1, source_target_pairs={{0,1},{1,2},{2,3},{3,4},{4,5},{5,6},{6,7},{7,8},{8,9},{9,10},{10,1... | collective-permute-start | bytes 196616 | tf_op jit(solution)/shard_map/halos/ppermute | solution.py:202
  41.7 5.5 %collective-permute-start.5 = (f32[32,4,128]{2,1,0:T(4,128)S(1)}, f32[32,4,128]{2,1,0:T(4,128)S(1)}, u32[]{:S(2)}, u32[]{:S(2)}) collective-permute-start(f32[32,4,128]{2,1,0:T(4,128)S(1)} %pad_maximum_fusion.halo), channel_id=1, source_target_pairs={{1,0},{2,1},{3,2},{4,3},{5,4},{6,5},{7,6},{8,7},{9,8},{10,9},{11,1... | collective-permute-start | bytes 196616 | tf_op jit(solution)/shard_map/halos/ppermute | solution.py:203

commit v2 on v1

v2 whole, which is shorter than its diff:
```python
import math

import jax
import jax.numpy as jnp
import ml_dtypes
import numpy as np
from jax import lax
from jax.experimental import pallas as pl
from jax.experimental.pallas import tpu as pltpu
from jax.sharding import PartitionSpec as P

NLON = 2048
BLK = 128
NBLK = NLON // BLK
HL = 2
PROWS = 8
F32 = jnp.float32
BF16 = jnp.bfloat16


def cubic_weights(position):
    return (
        -position * (position - 1.0) * (position - 2.0) / 6.0,
        (position + 1.0) * (position - 1.0) * (position - 2.0) / 2.0,
        -(position + 1.0) * position * (position - 2.0) / 2.0,
        (position + 1.0) * position * (position - 1.0) / 6.0,
    )


def cubic_limited(values, cells, weights):
    def at(shift):
        return jnp.take_along_axis(values, cells + shift, axis=1, mode="promise_in_bounds")

    before_one, at_anchor, after_one, after_two = at(-1), at(0), at(1), at(2)
    interpolated = (
        weights[0] * before_one
        + weights[1] * at_anchor
        + weights[2] * after_one
        + weights[3] * after_two
    )
    lowest_bound = jnp.minimum(at_anchor, after_one)
    upper_bound = jnp.maximum(at_anchor, after_one)
    return jnp.minimum(jnp.maximum(interpolated, lowest_bound), upper_bound)


def two_pieces(table):
    high = table.astype(ml_dtypes.bfloat16)
    return high, (table - high.astype(np.float64)).astype(ml_dtypes.bfloat16)


def fourier_tables():
    b = np.arange(NBLK)
    angles = 2.0 * math.pi * np.outer(b, b) / NBLK
    rows = np.eye(PROWS)
    blocks = np.concatenate([np.kron(np.cos(angles), rows), -np.kron(np.sin(angles), rows)], 0)
    i = np.arange(BLK)
    angles = 2.0 * math.pi * (np.outer(i, i) % BLK) / BLK
    cosine, sine = np.cos(angles), np.sin(angles)
    cells = np.block([[cosine, -sine], [sine, cosine]])
    angles = 2.0 * math.pi * np.repeat(np.outer(b, i), PROWS, 0) / NLON
    turn = np.stack([np.cos(angles), -np.sin(angles)]).astype(np.float32)
    return (*two_pieces(blocks), *two_pieces(blocks.T.copy()), *two_pieces(cells), turn)


def dot(left, right):
    return jnp.dot(left, right, preferred_element_type=F32)


def split(values):
    high = values.astype(BF16)
    return high, (values - high.astype(F32)).astype(BF16)


def pack_kernel(source, tracer, offset, fraction, out, block, slab, cells, aux, sems):
    channels, rows = tracer.shape[0], tracer.shape[1]
    first = jnp.where(lax.axis_index("lat") == 0, 0, rows - PROWS)
    own = pl.ds(pl.multiple_of(first, PROWS), PROWS)
    copies = [
        pltpu.make_async_copy(source, block, sems.at[0]),
        pltpu.make_async_copy(offset.at[own, :], cells, sems.at[1]),
        pltpu.make_async_copy(fraction.at[own, :], aux.at[0, 1], sems.at[2]),
        pltpu.make_async_copy(tracer.at[:, own, :], slab, sems.at[3]),
    ]
    for copy in copies:
        copy.start()
    for copy in copies[:3]:
        copy.wait()
    spread = jnp.broadcast_to(block[...], (PROWS, rows))
    row = first + lax.broadcasted_iota(jnp.int32, (PROWS, rows), 0)
    mine = row == lax.broadcasted_iota(jnp.int32, (PROWS, rows), 1)
    source_block = jnp.sum(jnp.where(mine, spread, 0), axis=1, keepdims=True)
    anchor = (source_block * BLK + cells[...]).astype(F32)
    position = aux[0, 1]
    for n in range(NBLK):
        aux[n, 0] = anchor
        aux[n, 1] = position
    beside = pltpu.make_async_copy(aux, out.at[:, 2:4], sems.at[4])
    beside.start()
    copies[3].wait()
    share = slab.reshape(NBLK, channels // NBLK, PROWS, BLK)
    band = pltpu.make_async_copy(share, out.at[:, 0:2], sems.at[5])
    band.start()
    beside.wait()
    band.wait()


def polar_kernel(
    band, weights, blocks_h, blocks_l, back_h, back_l, cells_h, cells_l, turn, out
):
    count = NBLK * PROWS
    anchor = band[:, 2].reshape(count, BLK).astype(jnp.int32)
    place = ((anchor >> 7) & 15) * PROWS + ((anchor >> 11) & 7)
    lanes = lax.broadcasted_iota(jnp.int32, (count, BLK), 1)
    chosen = jnp.where(place == lanes, 1.0, 0.0).astype(BF16)
    own = jnp.concatenate([band[:, 0].reshape(count, BLK), band[:, 1].reshape(count, BLK)], 1)
    high = own.astype(BF16)
    rest = own - high.astype(F32)
    middle = rest.astype(BF16)
    low = (rest - middle.astype(F32)).astype(BF16)
    picked = dot(chosen, high) + dot(chosen, middle) + dot(chosen, low)
    cell = anchor & 127
    cubic = cubic_weights(band[:, 3].reshape(count, BLK))
    limited = [
        cubic_limited(picked[:, :BLK], cell, cubic),
        cubic_limited(picked[:, BLK:], cell, cubic),
    ]
    turn_r, turn_i = turn[0], turn[1]
    high, low = split(jnp.concatenate(limited, 1))
    first = dot(blocks_h[...], high) + dot(blocks_h[...], low) + dot(blocks_l[...], high)
    parts = []
    for c in range(2):
        real, imag = first[:count, c * BLK : (c + 1) * BLK], first[count:, c * BLK : (c + 1) * BLK]
        parts.append(
            jnp.concatenate([real * turn_r - imag * turn_i, real * turn_i + imag * turn_r], 1)
        )
    high, low = split(jnp.concatenate(parts, 0))
    spectrum = dot(high, cells_h[...]) + dot(low, cells_h[...]) + dot(high, cells_l[...])
    damping = jnp.concatenate([weights[...], weights[...]], 0)
    damped = jnp.concatenate([spectrum[:, BLK:] * damping, spectrum[:, :BLK] * damping], 1)
    high, low = split(damped)
    second = dot(high, cells_h[...]) + dot(low, cells_h[...]) + dot(high, cells_l[...])
    reals, imags = [], []
    for c in range(2):
        imag, real = second[c * count : (c + 1) * count, :BLK], second[c * count : (c + 1) * count, BLK:]
        reals.append(real * turn_r + imag * turn_i)
        imags.append(imag * turn_r - real * turn_i)
    high, low = split(
        jnp.concatenate([jnp.concatenate(reals, 1), jnp.concatenate(imags, 1)], 0)
    )
    removed = dot(back_h[...], high) + dot(back_h[...], low) + dot(back_l[...], high)
    for c in range(2):
        kept = limited[c] - removed[:, c * BLK : (c + 1) * BLK]
        out[:, c] = kept.reshape(NBLK, PROWS, BLK)


def column_rows(columns, first):
    channels, rows = columns[0].shape[0], columns[0].shape[1]
    flat = [column.reshape(channels * rows, BLK) for column in columns]
    return [part[pl.ds(first, channels, stride=rows), :] for part in flat]


def store_row(out, j, values):
    channels, rows = out.shape[0], out.shape[1]
    out.reshape(channels * rows, BLK)[pl.ds(j, channels, stride=rows), :] = values


def own_values(columns, column, row):
    west, own, east = column_rows(columns, jnp.clip(row, 0, columns[0].shape[1] - 1))
    return jnp.where(column == 0, west, jnp.where(column == 1, own, east))


def store_border(columns, lower, out):
    first = jnp.where(lower, columns[0].shape[1] - HL, 0)
    for j in range(HL):
        for n, values in enumerate(column_rows(columns, first + j)):
            out[n, j] = values


def border_kernel(west, own, east, out):
    store_border((west, own, east), lax.axis_index("lat") % 2 == 1, out)


def row_values(columns, column, row, beyond, halo):
    beyond = jnp.clip(beyond, 0, HL - 1)
    outside = (row < 0) | (row >= columns[0].shape[1])
    return jnp.where(outside, halo[column, beyond], own_values(columns, column, row))


def rows_kernel(place, offset, fraction, west, own, east, other, out, to_pair, cubic):
    first_of_pair = lax.axis_index("lat") % 2 == 0
    channels, rows = own.shape[0], own.shape[1]
    columns = (west, own, east)
    store_border(columns, first_of_pair, to_pair)
    for n, weight in enumerate(cubic_weights(fraction[...])):
        cubic[n] = weight
    for j in range(rows):
        column, row = place[0, j], place[1, j]
        if HL <= j < rows - HL:
            values = own_values(columns, column, row)
        else:
            values = row_values(columns, column, row, row + HL if j < HL else row - rows, other)
        cells = jnp.broadcast_to(offset[j : j + 1, :], (channels, BLK))
        weights = [cubic[n, j : j + 1, :] for n in range(4)]
        store_row(out, j, cubic_limited(values, cells, weights))


def edge_kernel(place, offset, fraction, west, own, east, pair, rows_done, out):
    del rows_done
    first_of_pair = lax.axis_index("lat") % 2 == 0
    channels, rows = own.shape[0], own.shape[1]
    first = jnp.where(first_of_pair, rows - HL, 0)
    for j in range(HL):
        column, row = place[0, first + j], place[1, first + j]
        beyond = jnp.where(first_of_pair, row - rows, row + HL)
        values = row_values((west, own, east), column, row, beyond, pair)
        here = pl.ds(first + j, 1)
        cells = jnp.broadcast_to(offset[here, :], (channels, BLK))
        store_row(out, first + j, cubic_limited(values, cells, cubic_weights(fraction[here, :])))


def merge_kernel(rows_done, polar, out, sems):
    lat = lax.axis_index("lat")
    last = lax.axis_size("lat") - 1
    rows = out.shape[1]

    def copy(source, first, count, n):
        span = pl.ds(first, count)
        part = source if source is polar else source.at[:, span, :]
        return pltpu.make_async_copy(part, out.at[:, span, :], sems.at[n])

    middle = copy(rows_done, PROWS, rows - 2 * PROWS, 0)
    middle.start()
    for n, (first, side) in enumerate(((0, 0), (rows - PROWS, last))):

        @pl.when(lat == side)
        def _():
            copy(polar, first, PROWS, n + 1).start()

        @pl.when(lat != side)
        def _():
            copy(rows_done, first, PROWS, n + 1).start()

    middle.wait()
    for n, first in enumerate((0, rows - PROWS)):
        copy(rows_done, first, PROWS, n + 1).wait()


def body(tracer, source, offset, fraction, cutoffs):
    channels, rows, cells = tracer.shape
    lat_count = lax.axis_size("lat")
    lat, lon = lax.axis_index("lat"), lax.axis_index("lon")
    blocks = source.reshape(rows)

    smem = pl.BlockSpec(memory_space=pltpu.SMEM)
    vmem = pl.BlockSpec(memory_space=pltpu.VMEM)
    anyplace = pl.BlockSpec(memory_space=pl.ANY)
    field = jax.ShapeDtypeStruct(tracer.shape, F32)

    def call(kernel, out_shape, in_specs, out_specs, scratch, limit, flops, **more):
        return pl.pallas_call(
            kernel,
            out_shape=out_shape,
            in_specs=in_specs,
            out_specs=out_specs,
            scratch_shapes=scratch,
            compiler_params=pltpu.CompilerParams(vmem_limit_bytes=limit << 20),
            cost_estimate=pl.CostEstimate(
                flops=flops, bytes_accessed=1 << 20, transcendentals=0
            ),
            **more,
        )

    def moved(values, target):
        pairs = []
        for a in range(lat_count):
            for b in range(NBLK):
                to = target(a, b)
                if 0 <= to[0] < lat_count:
                    pairs.append((a * NBLK + b, to[0] * NBLK + to[1] % NBLK))
        return lax.ppermute(values, ("lat", "lon"), pairs)

    dma = pltpu.SemaphoreType.DMA
    with jax.named_scope("lon_neighbours"):
        west = moved(tracer, lambda a, b: (a, b + 1))
        east = moved(tracer, lambda a, b: (a, b - 1))

    def filter_band():
        packed = call(
            pack_kernel,
            jax.ShapeDtypeStruct((NBLK, 4, PROWS, BLK), F32),
            [anyplace] * 4,
            anyplace,
            [
                pltpu.VMEM((1, rows), jnp.int32),
                pltpu.VMEM((channels, PROWS, BLK), F32),
                pltpu.VMEM((PROWS, BLK), jnp.int32),
                pltpu.VMEM((NBLK, 2, PROWS, BLK), F32),
                dma((6,)),
            ],
            60,
            1_000_000,
        )(source.reshape(1, rows), tracer, offset, fraction)
        band = lax.all_to_all(packed, "lon", 0, 0)
        kappa = jnp.where(lat == 0, cutoffs[0], cutoffs[1]).astype(F32)
        k1 = jnp.arange(NBLK, dtype=jnp.int32)
        k2 = jnp.arange(BLK, dtype=jnp.int32)
        wave = k1[:, None, None] + NBLK * k2[None, None, :]
        wave = jnp.minimum(wave, NLON - wave)
        inside = (wave >= 1) & (wave < NLON // 2)
        ratio = kappa[None, :, None] / jnp.maximum(wave, 1).astype(F32)
        damping = jnp.where(inside, jnp.maximum(1.0 - ratio, 0.0), 0.0) * (1.0 / NLON)
        return call(
            polar_kernel,
            jax.ShapeDtypeStruct((NBLK, 2, PROWS, BLK), F32),
            [vmem] * 9,
            vmem,
            [],
            16,
            400_000_000,
        )(band, damping.reshape(NBLK * PROWS, BLK), *fourier_tables())

    with jax.named_scope("polar_rows"):
        filtered = lax.cond(
            (lat == 0) | (lat == lat_count - 1),
            filter_band,
            lambda: jnp.zeros((NBLK, 2, PROWS, BLK), F32),
        )
        polar = lax.all_to_all(filtered, "lon", 0, 0).reshape(channels, PROWS, BLK)

    with jax.named_scope("borders"):
        border = jax.ShapeDtypeStruct((3, HL, channels, cells), F32)
        to_other = call(border_kernel, border, [vmem] * 3, vmem, [], 16, 1_000_000)(
            west, tracer, east
        )
        other = moved(to_other, lambda a, b: (a + (1 if a % 2 else -1), b))

    with jax.named_scope("other_rows"):
        row = blocks // NBLK - lat * rows
        column = jnp.clip(jnp.mod(blocks % NBLK - lon + 1, NBLK), 0, 2)
        place = jnp.stack([column, row])
        inner_done, to_pair = call(
            rows_kernel,
            (field, border),
            [smem] + [vmem] * 6,
            (vmem, vmem),
            [pltpu.VMEM((4, rows, BLK), F32)],
            16,
            3_000_000_000,
        )(place, offset, fraction, west, tracer, east, other)
        pair = moved(to_pair, lambda a, b: (a + (-1 if a % 2 else 1), b))
        done = call(
            edge_kernel,
            field,
            [smem] + [vmem] * 7,
            vmem,
            [],
            16,
            1_000_000,
            input_output_aliases={7: 0},
        )(place, offset, fraction, west, tracer, east, pair, inner_done)

    with jax.named_scope("merge"):
        return call(
            merge_kernel,
            field,
            [anyplace, anyplace],
            anyplace,
            [dma((3,))],
            4,
            1_000_000,
        )(done, polar)


def solution(mesh):
    placed = (P(None, "lat", "lon"), P("lat", "lon"), P("lat", "lon"), P("lat", "lon"), P())
    return jax.shard_map(
        body, mesh=mesh, in_specs=placed, out_specs=P(None, "lat", "lon"), check_vma=False
    )
```

time: 50.4 us -> 41.8 us (0.83)
  the two profiles are of different devices: /device:TPU:4 before, /device:TPU:32 now
where the time goes in v2:
time: 41.8 us; the launch traced here: 41.4 us
  starting transfers between devices  18.5 us (44%)
  waiting for transfers between devices  12.6 us (30%)
  Pallas kernels  9.2 us (22%)
  local copies, waits for them, and re-layouts  0.83 us (2%)
    all_to_all x1, starting transfers between devices, filter_band(): band = lax.all_to_all(packed, 'lon', 0, 0)  11 us
    all_to_all x1, waiting for transfers between devices, filter_band(): band = lax.all_to_all(packed, 'lon', 0, 0)  9.77 us
    all_to_all x1, starting transfers between devices, body(): polar = lax.all_to_all(filtered, 'lon', 0, 0).reshape(channels, PROWS, BLK)  4.72 us
    ppermute x4, starting transfers between devices, moved(): return lax.ppermute(values, ('lat', 'lon'), pairs)  2.79 us
    pallas_call x1, Pallas kernels, filter_band(): call(polar_kernel, jax.ShapeDtypeStruct((NBLK, 2, PROWS, BLK), F32), [vme...  2.4 us
    pallas_call x1, Pallas kernels, body(): call(rows_kernel, (field, border), [smem] + [vmem] * 6, (vmem, vmem), [pl...  2.38 us
    pallas_call x1, Pallas kernels, filter_band(): call(pack_kernel, jax.ShapeDtypeStruct((NBLK, 4, PROWS, BLK), F32), [anyp...  1.66 us
    all_to_all x1, waiting for transfers between devices, body(): polar = lax.all_to_all(filtered, 'lon', 0, 0).reshape(channels, PROWS, BLK)  1.49 us
  transfers between devices with their start and end apart: 6, of which 3 were waited for; matrix products, arithmetic and copies ran while one was open for 1% of the time, Pallas kernels for 20%

profile of v2, /device:TPU:32, one launch (start us, length us, event | category | flops | bytes accessed | tf_op | source)
XLA Modules:
  0.0 41.4 jit_solution(12140556772346213525)
XLA Ops:
  0.0 1.9 %collective-permute-start = (f32[32,32,128]{2,1,0:T(8,128)}, f32[32,32,128]{2,1,0:T(8,128)S(1)}, u32[]{:S(2)}, u32[]{:S(2)}) collective-permute-start(f32[32,32,128]{2,1,0:T(8,128)} %own.5), channel_id=1, source_target_pairs={{0,1},{1,2},{2,3},{3,4},{4,5},{5,6},{6,7},{7,8},{8,9},{9,10},{10,1... | collective-permute-start | bytes 1572872 | tf_op jit(solution)/shard_map/lon_neighbours/ppermute | solution.py:280
  1.9 0.1 collective-permute-start.1
  2.0 0.0 copy-done.8
  2.0 0.6 %copy-done.10 = s32[32,1]{0,1:T(1,128)S(1)} copy-done((s32[32,1]{0,1:T(1,128)S(1)}, s32[32,1]{0,1:T(1,128)}, u32[]{:S(2)}) %copy-start.10) | copy-done | bytes 152
  2.7 0.0 copy-done.11
  2.7 25.2 %conditional.1 = (f32[16,2,8,128]{3,2,1,0:T(8,128)}) conditional(s32[]{:T(128)} %convert_element_type.21, () %tuple.11, (s32[32,1]{0,1:T(1,128)S(1)}, f32[32,32,128]{2,1,0:T(8,128)}, s32[32,128]{1,0:T(8,128)S(1)}, f32[32,128]{1,0:T(8,128)}, s32[]{:T(128)}, /*index=5*/s32[2,8]{1,0:T(2,128)S(1)}, (), (), (), (), /*index=10*/(), (), ()) %tuple.46), branch_computations={%region_0.0_spmd, %region_1.2_spmd} | conditional | flops 401104608 | bytes 5594998 | solution.py:323
  2.7 1.7 %branch_1_fun.2 = f32[16,4,8,128]{3,2,1,0:T(8,128)} custom-call(s32[1,32]{1,0:T(1,128)S(1)} %bitcast.34, f32[32,32,128]{2,1,0:T(8,128)} %get-tuple-element.35.tracer, s32[32,128]{1,0:T(8,128)S(1)} %get-tuple-element.36.offset, f32[32,128]{1,0:T(8,128)} %get-tuple-element.37.fraction), custom_call_target="tpu_custom_call" | custom-call | flops 1000000 | bytes 1048576 | tf_op jit(solution)/shard_map/polar_rows/cond/branch_1_fun/pallas_call | solution.py:288
  4.4 0.0 copy-start
  4.4 0.0 copy-start.1
  4.4 0.0 copy-start.2
  4.4 0.0 copy-start.4
  4.4 0.0 copy-start.5
  4.5 11.0 %all-to-all-start = ((f32[16,4,8,128]{3,2,1,0:T(8,128)}), f32[16,4,8,128]{3,2,1,0:T(8,128)S(1)}, u32[]{:S(2)}, u32[]{:S(2)}) async-start(f32[16,4,8,128]{3,2,1,0:T(8,128)} %branch_1_fun.2), calls=%async_computation | async-start | bytes 524288 | tf_op jit(solution)/shard_map/polar_rows/cond/branch_1_fun/all_to_all | solution.py:303
  15.5 0.1 div.23
  15.6 0.1 fusion.3.weights
  15.7 9.8 %all-to-all-done.band = f32[16,4,8,128]{3,2,1,0:T(8,128)S(1)} async-done(((f32[16,4,8,128]{3,2,1,0:T(8,128)}), f32[16,4,8,128]{3,2,1,0:T(8,128)S(1)}, u32[]{:S(2)}, u32[]{:S(2)}) %all-to-all-start) | async-done | bytes 262176 | tf_op jit(solution)/shard_map/polar_rows/cond/branch_1_fun/all_to_all | solution.py:303
  25.4 0.0 copy-done.6
  25.5 2.4 %branch_1_fun.3 = f32[16,2,8,128]{3,2,1,0:T(8,128)} custom-call(f32[16,4,8,128]{3,2,1,0:T(8,128)S(1)} %all-to-all-done.band, f32[128,128]{1,0:T(8,128)S(1)} %fusion.3.weights, bf16[256,128]{1,0:T(8,128)(2,1)S(1)} %copy-done.3, bf16[256,128]{1,0:T(8,128)(2,1)S(1)} %copy-done.4, bf16[128,256]{1,0:T(8,128)(2,1)S(1)} %copy-done.5, ...), custom_call_target="tpu_custom_call" | custom-call | flops 400000000 | bytes 1048576 | tf_op jit(solution)/shard_map/polar_rows/cond/branch_1_fun/pallas_call | solution.py:312
  27.9 4.7 %all-to-all-start.1 = ((f32[16,2,8,128]{3,2,1,0:T(8,128)}), f32[16,2,8,128]{3,2,1,0:T(8,128)S(1)}, u32[]{:S(2)}, u32[]{:S(2)}) async-start(f32[16,2,8,128]{3,2,1,0:T(8,128)} %get-tuple-element.69), calls=%async_computation.1 | async-start | bytes 262144 | tf_op jit(solution)/shard_map/polar_rows/all_to_all | solution.py:328
  32.6 0.0 copy-start.7
  32.6 0.0 copy-start.9
  32.7 0.0 collective-permute-done.west
  32.7 0.0 collective-permute-done.1.east
  32.7 1.2 %borders.1 = f32[3,2,32,128]{3,2,1,0:T(8,128)S(1)} custom-call(f32[32,32,128]{2,1,0:T(8,128)S(1)} %collective-permute-done.west, f32[32,32,128]{2,1,0:T(8,128)} %own.5, f32[32,32,128]{2,1,0:T(8,128)S(1)} %collective-permute-done.1.east), custom_call_target="tpu_custom_call" | custom-call | flops 1000000 | bytes 1048576 | tf_op jit(solution)/shard_map/borders/pallas_call | solution.py:332
  33.9 0.7 %collective-permute-start.2 = (f32[3,2,32,128]{3,2,1,0:T(8,128)S(1)}, f32[3,2,32,128]{3,2,1,0:T(8,128)S(1)}, u32[]{:S(2)}, u32[]{:S(2)}) collective-permute-start(f32[3,2,32,128]{3,2,1,0:T(8,128)S(1)} %borders.1), channel_id=1, source_target_pairs={{16,32},{17,33},{18,34},{19,35},{20,36},{21,37},{22,38},{23,39},{2... | collective-permute-start | bytes 294920 | tf_op jit(solution)/shard_map/borders/ppermute | solution.py:280
  34.5 0.0 collective-permute-done.2.other
  34.6 2.4 %other_rows.2 = (f32[32,32,128]{2,1,0:T(8,128)S(1)}, f32[3,2,32,128]{3,2,1,0:T(8,128)S(1)}) custom-call(s32[2,32]{1,0:T(2,128)S(1)} %pad_add_fusion.place, s32[32,128]{1,0:T(8,128)S(1)} %copy-done.8, f32[32,128]{1,0:T(8,128)S(1)} %copy-done.9, f32[32,32,128]{2,1,0:T(8,128)S(1)} %collective-permute-done.west, f32[32,32,128]{2,1,0:T(8,128)S(1)} %copy-done.7, ...), custom_call_target="tpu_custom_call" | custom-call | flops 3000000000 | bytes 1048576 | tf_op jit(solution)/shard_map/other_rows/pallas_call | solution.py:341
  37.0 0.1 collective-permute-start.3
  37.1 1.3 %collective-permute-done.3.pair = f32[3,2,32,128]{3,2,1,0:T(8,128)S(1)} collective-permute-done((f32[3,2,32,128]{3,2,1,0:T(8,128)S(1)}, f32[3,2,32,128]{3,2,1,0:T(8,128)S(1)}, u32[]{:S(2)}, u32[]{:S(2)}) %collective-permute-start.3) | collective-permute-done | bytes 98336 | tf_op jit(solution)/shard_map/other_rows/ppermute | solution.py:280
  38.4 0.8 %other_rows.3.rows_done = f32[32,32,128]{2,1,0:T(8,128)S(1)} custom-call(s32[2,32]{1,0:T(2,128)S(1)} %pad_add_fusion.place, s32[32,128]{1,0:T(8,128)S(1)} %copy-done.8, f32[32,128]{1,0:T(8,128)S(1)} %copy-done.9, f32[32,32,128]{2,1,0:T(8,128)S(1)} %collective-permute-done.west, f32[32,32,128]{2,1,0:T(8,128)S(1)} %copy-done.7, ...), custom_call_target="tpu_custom_call", output_to_operand_aliasing={{}: (7, {})} | custom-call | flops 1000000 | bytes 1048576 | tf_op jit(solution)/shard_map/other_rows/pallas_call | solution.py:351
  39.1 1.5 %all-to-all-done.1 = f32[16,2,8,128]{3,2,1,0:T(8,128)S(1)} async-done(((f32[16,2,8,128]{3,2,1,0:T(8,128)}), f32[16,2,8,128]{3,2,1,0:T(8,128)S(1)}, u32[]{:S(2)}, u32[]{:S(2)}) %all-to-all-start.1) | async-done | bytes 131104 | tf_op jit(solution)/shard_map/polar_rows/all_to_all | solution.py:328
  40.6 0.8 %merge.1 = f32[32,32,128]{2,1,0:T(8,128)} custom-call(f32[32,32,128]{2,1,0:T(8,128)S(1)} %other_rows.3.rows_done, f32[32,8,128]{2,1,0:T(8,128)S(1)} %bitcast.33), custom_call_target="tpu_custom_call" | custom-call | flops 1000000 | bytes 1048576 | tf_op jit(solution)/shard_map/merge/pallas_call | solution.py:363
  (20 shorter events, 0.1 us)
Async XLA Ops:
  0.0 2.0 %copy-start.8 = (s32[32,128]{1,0:T(8,128)S(1)}, s32[32,128]{1,0:T(8,128)}, u32[]{:S(2)}) copy-start(s32[32,128]{1,0:T(8,128)} %offset.3) | copy-start | bytes 49156
  0.0 32.7 %collective-permute-start = (f32[32,32,128]{2,1,0:T(8,128)}, f32[32,32,128]{2,1,0:T(8,128)S(1)}, u32[]{:S(2)}, u32[]{:S(2)}) collective-permute-start(f32[32,32,128]{2,1,0:T(8,128)} %own.5), channel_id=1, source_target_pairs={{0,1},{1,2},{2,3},{3,4},{4,5},{5,6},{6,7},{7,8},{8,9},{9,10},{10,1... | collective-permute-start | bytes 1572872 | tf_op jit(solution)/shard_map/lon_neighbours/ppermute | solution.py:280
  1.9 30.7 %collective-permute-start.1 = (f32[32,32,128]{2,1,0:T(8,128)}, f32[32,32,128]{2,1,0:T(8,128)S(1)}, u32[]{:S(2)}, u32[]{:S(2)}) collective-permute-start(f32[32,32,128]{2,1,0:T(8,128)} %own.5), channel_id=1, source_target_pairs={{0,15},{1,0},{2,1},{3,2},{4,3},{5,4},{6,5},{7,6},{8,7},{9,8},{10,9... | collective-permute-start | bytes 1572872 | tf_op jit(solution)/shard_map/lon_neighbours/ppermute | solution.py:280
  2.0 0.7 %copy-start.10 = (s32[32,1]{0,1:T(1,128)S(1)}, s32[32,1]{0,1:T(1,128)}, u32[]{:S(2)}) copy-start(s32[32,1]{0,1:T(1,128)} %param.15) | copy-start | bytes 388
  2.0 0.7 %copy-start.11 = (s32[2,8]{1,0:T(2,128)S(1)}, s32[2,8]{1,0:T(2,128)}, u32[]{:S(2)}) copy-start(s32[2,8]{1,0:T(2,128)} %param.18) | copy-start | bytes 196
  2.7 22.7 %copy-start.6 = (bf16[128,256]{1,0:T(8,128)(2,1)S(1)}, bf16[128,256]{1,0:T(8,128)(2,1)}, u32[]{:S(2)}) copy-start(bf16[128,256]{1,0:T(8,128)(2,1)} %constant.83.clone.1.back_l) | copy-start | bytes 196612 | tf_op jit(solution)/shard_map/polar_rows/cond
  4.4 21.1 %copy-start = (bf16[256,256]{1,0:T(8,128)(2,1)S(1)}, bf16[256,256]{1,0:T(8,128)(2,1)}, u32[]{:S(2)}) copy-start(bf16[256,256]{1,0:T(8,128)(2,1)} %constant.84.clone.1.cells_h) | copy-start | bytes 393220 | tf_op jit(solution)/shard_map/polar_rows/cond
  4.4 21.0 %copy-start.1 = (bf16[256,256]{1,0:T(8,128)(2,1)S(1)}, bf16[256,256]{1,0:T(8,128)(2,1)}, u32[]{:S(2)}) copy-start(bf16[256,256]{1,0:T(8,128)(2,1)} %constant.85.clone.1.cells_l) | copy-start | bytes 393220 | tf_op jit(solution)/shard_map/polar_rows/cond
  4.4 21.0 %copy-start.2 = (f32[2,128,128]{2,1,0:T(8,128)S(1)}, f32[2,128,128]{2,1,0:T(8,128)}, u32[]{:S(2)}) copy-start(f32[2,128,128]{2,1,0:T(8,128)} %constant.86.clone.1.turn) | copy-start | bytes 393220 | tf_op jit(solution)/shard_map/polar_rows/cond
  4.4 21.0 %copy-start.4 = (bf16[256,128]{1,0:T(8,128)(2,1)S(1)}, bf16[256,128]{1,0:T(8,128)(2,1)}, u32[]{:S(2)}) copy-start(bf16[256,128]{1,0:T(8,128)(2,1)} %constant.81.clone.1.blocks_l) | copy-start | bytes 196612 | tf_op jit(solution)/shard_map/polar_rows/cond
  4.4 21.0 %copy-start.5 = (bf16[128,256]{1,0:T(8,128)(2,1)S(1)}, bf16[128,256]{1,0:T(8,128)(2,1)}, u32[]{:S(2)}) copy-start(bf16[128,256]{1,0:T(8,128)(2,1)} %constant.82.clone.1.back_h) | copy-start | bytes 196612 | tf_op jit(solution)/shard_map/polar_rows/cond
  4.5 21.0 %all-to-all-start = ((f32[16,4,8,128]{3,2,1,0:T(8,128)}), f32[16,4,8,128]{3,2,1,0:T(8,128)S(1)}, u32[]{:S(2)}, u32[]{:S(2)}) async-start(f32[16,4,8,128]{3,2,1,0:T(8,128)} %branch_1_fun.2), calls=%async_computation | async-start | bytes 524288 | tf_op jit(solution)/shard_map/polar_rows/cond/branch_1_fun/all_to_all | solution.py:303
  15.4 10.1 %copy-start.3 = (bf16[256,128]{1,0:T(8,128)(2,1)S(1)}, bf16[256,128]{1,0:T(8,128)(2,1)}, u32[]{:S(2)}) copy-start(bf16[256,128]{1,0:T(8,128)(2,1)} %constant.80.clone.1.blocks_h) | copy-start | bytes 196612 | tf_op jit(solution)/shard_map/polar_rows/cond
  27.9 12.7 %all-to-all-start.1 = ((f32[16,2,8,128]{3,2,1,0:T(8,128)}), f32[16,2,8,128]{3,2,1,0:T(8,128)S(1)}, u32[]{:S(2)}, u32[]{:S(2)}) async-start(f32[16,2,8,128]{3,2,1,0:T(8,128)} %get-tuple-element.69), calls=%async_computation.1 | async-start | bytes 262144 | tf_op jit(solution)/shard_map/polar_rows/all_to_all | solution.py:328
  32.6 1.9 %copy-start.7 = (f32[32,32,128]{2,1,0:T(8,128)S(1)}, f32[32,32,128]{2,1,0:T(8,128)}, u32[]{:S(2)}) copy-start(f32[32,32,128]{2,1,0:T(8,128)} %own.5) | copy-start | bytes 1572868
  32.6 1.9 %copy-start.9 = (f32[32,128]{1,0:T(8,128)S(1)}, f32[32,128]{1,0:T(8,128)}, u32[]{:S(2)}) copy-start(f32[32,128]{1,0:T(8,128)} %fraction.3) | copy-start | bytes 49156
  33.9 0.7 %collective-permute-start.2 = (f32[3,2,32,128]{3,2,1,0:T(8,128)S(1)}, f32[3,2,32,128]{3,2,1,0:T(8,128)S(1)}, u32[]{:S(2)}, u32[]{:S(2)}) collective-permute-start(f32[3,2,32,128]{3,2,1,0:T(8,128)S(1)} %borders.1), channel_id=1, source_target_pairs={{16,32},{17,33},{18,34},{19,35},{20,36},{21,37},{22,38},{23,39},{2... | collective-permute-start | bytes 294920 | tf_op jit(solution)/shard_map/borders/ppermute | solution.py:280
  37.0 1.4 %collective-permute-start.3 = (f32[3,2,32,128]{3,2,1,0:T(8,128)S(1)}, f32[3,2,32,128]{3,2,1,0:T(8,128)S(1)}, u32[]{:S(2)}, u32[]{:S(2)}) collective-permute-start(f32[3,2,32,128]{3,2,1,0:T(8,128)S(1)} %get-tuple-element.49), channel_id=1, source_target_pairs={{0,16},{1,17},{2,18},{3,19},{4,20},{5,21},{6,22},{7,23},{8,24},{9,... | collective-permute-start | bytes 294920 | tf_op jit(solution)/shard_map/other_rows/ppermute | solution.py:280

commit v3 on v2

--- a/solution.py
+++ b/solution.py
@@ -13,6 +13,7 @@
 BLK = 128
 NBLK = NLON // BLK
 HL = 2
+HALF = NBLK // 2 + 1
 PROWS = 8
 F32 = jnp.float32
 BF16 = jnp.bfloat16
@@ -45,21 +46,23 @@
 
 def two_pieces(table):
     high = table.astype(ml_dtypes.bfloat16)
-    return high, (table - high.astype(np.float64)).astype(ml_dtypes.bfloat16)
+    return np.stack([high, (table - high.astype(np.float64)).astype(ml_dtypes.bfloat16)])
 
 
 def fourier_tables():
-    b = np.arange(NBLK)
-    angles = 2.0 * math.pi * np.outer(b, b) / NBLK
+    b, k1 = np.arange(NBLK), np.arange(HALF)
+    angles = 2.0 * math.pi * np.outer(k1, b) / NBLK
     rows = np.eye(PROWS)
     blocks = np.concatenate([np.kron(np.cos(angles), rows), -np.kron(np.sin(angles), rows)], 0)
+    twice = np.where((k1 == 0) | (k1 == NBLK // 2), 1.0, 2.0)
+    back = blocks.T * np.tile(np.repeat(twice, PROWS), 2)[None, :]
     i = np.arange(BLK)
     angles = 2.0 * math.pi * (np.outer(i, i) % BLK) / BLK
     cosine, sine = np.cos(angles), np.sin(angles)
     cells = np.block([[cosine, -sine], [sine, cosine]])
-    angles = 2.0 * math.pi * np.repeat(np.outer(b, i), PROWS, 0) / NLON
+    angles = 2.0 * math.pi * np.repeat(np.outer(k1, i), PROWS, 0) / NLON
     turn = np.stack([np.cos(angles), -np.sin(angles)]).astype(np.float32)
-    return (*two_pieces(blocks), *two_pieces(blocks.T.copy()), *two_pieces(cells), turn)
+    return two_pieces(blocks), two_pieces(back), two_pieces(cells), turn
 
 
 def dot(left, right):
@@ -104,10 +107,29 @@
     band.wait()
 
 
-def polar_kernel(
-    band, weights, blocks_h, blocks_l, back_h, back_l, cells_h, cells_l, turn, out
-):
+def prepare_kernel(cutoffs, *refs):
+    tables, damping, held = refs[:4], refs[4], refs[5:]
+    for table, copy in zip(tables, held):
+        copy[...] = table[...]
+    shape = (HALF * PROWS, BLK)
+    row = lax.broadcasted_iota(jnp.int32, shape, 0)
+    wave = (row >> 3) + NBLK * lax.broadcasted_iota(jnp.int32, shape, 1)
+    wave = jnp.minimum(wave, NLON - wave)
+    side = jnp.where(lax.axis_index("lat") == 0, 0, 1)
+    kappa = jnp.zeros(shape, jnp.int32)
+    for j in range(PROWS):
+        kappa = jnp.where((row & (PROWS - 1)) == j, cutoffs[side, j], kappa)
+    inside = (wave >= 1) & (wave < NLON // 2)
+    ratio = kappa.astype(F32) / jnp.maximum(wave, 1).astype(F32)
+    damping[...] = jnp.where(inside, jnp.maximum(1.0 - ratio, 0.0), 0.0) * (1.0 / NLON)
+
+
+def polar_kernel(band, weights, blocks, back, cells, turn, out):
+    blocks_h, blocks_l = blocks[0], blocks[1]
+    back_h, back_l = back[0], back[1]
+    cells_h, cells_l = cells[0], cells[1]
     count = NBLK * PROWS
+    half = HALF * PROWS
     anchor = band[:, 2].reshape(count, BLK).astype(jnp.int32)
     place = ((anchor >> 7) & 15) * PROWS + ((anchor >> 11) & 7)
     lanes = lax.broadcasted_iota(jnp.int32, (count, BLK), 1)
@@ -126,28 +148,28 @@
     ]
     turn_r, turn_i = turn[0], turn[1]
     high, low = split(jnp.concatenate(limited, 1))
-    first = dot(blocks_h[...], high) + dot(blocks_h[...], low) + dot(blocks_l[...], high)
+    first = dot(blocks_h, high) + dot(blocks_h, low) + dot(blocks_l, high)
     parts = []
     for c in range(2):
-        real, imag = first[:count, c * BLK : (c + 1) * BLK], first[count:, c * BLK : (c + 1) * BLK]
+        real, imag = first[:half, c * BLK : (c + 1) * BLK], first[half:, c * BLK : (c + 1) * BLK]
         parts.append(
             jnp.concatenate([real * turn_r - imag * turn_i, real * turn_i + imag * turn_r], 1)
         )
     high, low = split(jnp.concatenate(parts, 0))
-    spectrum = dot(high, cells_h[...]) + dot(low, cells_h[...]) + dot(high, cells_l[...])
+    spectrum = dot(high, cells_h) + dot(low, cells_h) + dot(high, cells_l)
     damping = jnp.concatenate([weights[...], weights[...]], 0)
     damped = jnp.concatenate([spectrum[:, BLK:] * damping, spectrum[:, :BLK] * damping], 1)
     high, low = split(damped)
-    second = dot(high, cells_h[...]) + dot(low, cells_h[...]) + dot(high, cells_l[...])
+    second = dot(high, cells_h) + dot(low, cells_h) + dot(high, cells_l)
     reals, imags = [], []
     for c in range(2):
-        imag, real = second[c * count : (c + 1) * count, :BLK], second[c * count : (c + 1) * count, BLK:]
+        imag, real = second[c * half : (c + 1) * half, :BLK], second[c * half : (c + 1) * half, BLK:]
         reals.append(real * turn_r + imag * turn_i)
         imags.append(imag * turn_r - real * turn_i)
     high, low = split(
         jnp.concatenate([jnp.concatenate(reals, 1), jnp.concatenate(imags, 1)], 0)
     )
-    removed = dot(back_h[...], high) + dot(back_h[...], low) + dot(back_l[...], high)
+    removed = dot(back_h, high) + dot(back_h, low) + dot(back_l, high)
     for c in range(2):
         kept = limited[c] - removed[:, c * BLK : (c + 1) * BLK]
         out[:, c] = kept.reshape(NBLK, PROWS, BLK)
@@ -169,80 +191,59 @@
     return jnp.where(column == 0, west, jnp.where(column == 1, own, east))
 
 
-def store_border(columns, lower, out):
-    first = jnp.where(lower, columns[0].shape[1] - HL, 0)
+def border_kernel(west, own, east, *refs):
+    out = refs[-1]
+    to_other = len(refs) == 1
+    rows = own.shape[1]
+    lower = (lax.axis_index("lat") % 2 == 1) == to_other
+    first = jnp.where(lower, rows - HL, 0)
     for j in range(HL):
-        for n, values in enumerate(column_rows(columns, first + j)):
+        for n, values in enumerate(column_rows((west, own, east), first + j)):
             out[n, j] = values
-
-
-def border_kernel(west, own, east, out):
-    store_border((west, own, east), lax.axis_index("lat") % 2 == 1, out)
 
 
 def row_values(columns, column, row, beyond, halo):
     beyond = jnp.clip(beyond, 0, HL - 1)
     outside = (row < 0) | (row >= columns[0].shape[1])
-    return jnp.where(outside, halo[column, beyond], own_values(columns, column, row))
-
-
-def rows_kernel(place, offset, fraction, west, own, east, other, out, to_pair, cubic):
+    return jnp.where(outside, halo(column, beyond), own_values(columns, column, row))
+
+
+def rows_kernel(place, offset, fraction, west, own, east, other, pair, out, cubic):
     first_of_pair = lax.axis_index("lat") % 2 == 0
     channels, rows = own.shape[0], own.shape[1]
     columns = (west, own, east)
-    store_border(columns, first_of_pair, to_pair)
     for n, weight in enumerate(cubic_weights(fraction[...])):
         cubic[n] = weight
+
+    def north(column, row):
+        return jnp.where(first_of_pair, other[column, row], pair[column, row])
+
+    def south(column, row):
+        return jnp.where(first_of_pair, pair[column, row], other[column, row])
+
     for j in range(rows):
         column, row = place[0, j], place[1, j]
-        if HL <= j < rows - HL:
+        if j < HL:
+            values = row_values(columns, column, row, row + HL, north)
+        elif j < rows - HL:
             values = own_values(columns, column, row)
         else:
-            values = row_values(columns, column, row, row + HL if j < HL else row - rows, other)
+            values = row_values(columns, column, row, row - rows, south)
         cells = jnp.broadcast_to(offset[j : j + 1, :], (channels, BLK))
         weights = [cubic[n, j : j + 1, :] for n in range(4)]
         store_row(out, j, cubic_limited(values, cells, weights))
 
 
-def edge_kernel(place, offset, fraction, west, own, east, pair, rows_done, out):
-    del rows_done
-    first_of_pair = lax.axis_index("lat") % 2 == 0
-    channels, rows = own.shape[0], own.shape[1]
-    first = jnp.where(first_of_pair, rows - HL, 0)
-    for j in range(HL):
-        column, row = place[0, first + j], place[1, first + j]
-        beyond = jnp.where(first_of_pair, row - rows, row + HL)
-        values = row_values((west, own, east), column, row, beyond, pair)
-        here = pl.ds(first + j, 1)
-        cells = jnp.broadcast_to(offset[here, :], (channels, BLK))
-        store_row(out, first + j, cubic_limited(values, cells, cubic_weights(fraction[here, :])))
-
-
-def merge_kernel(rows_done, polar, out, sems):
+def merge_kernel(rows_done, polar, out, sem):
     lat = lax.axis_index("lat")
     last = lax.axis_size("lat") - 1
-    rows = out.shape[1]
-
-    def copy(source, first, count, n):
-        span = pl.ds(first, count)
-        part = source if source is polar else source.at[:, span, :]
-        return pltpu.make_async_copy(part, out.at[:, span, :], sems.at[n])
-
-    middle = copy(rows_done, PROWS, rows - 2 * PROWS, 0)
-    middle.start()
-    for n, (first, side) in enumerate(((0, 0), (rows - PROWS, last))):
-
-        @pl.when(lat == side)
-        def _():
-            copy(polar, first, PROWS, n + 1).start()
-
-        @pl.when(lat != side)
-        def _():
-            copy(rows_done, first, PROWS, n + 1).start()
-
-    middle.wait()
-    for n, first in enumerate((0, rows - PROWS)):
-        copy(rows_done, first, PROWS, n + 1).wait()
+
+    @pl.when((lat == 0) | (lat == last))
+    def _():
+        first = pl.multiple_of(jnp.where(lat == 0, 0, out.shape[1] - PROWS), PROWS)
+        copy = pltpu.make_async_copy(polar, out.at[:, pl.ds(first, PROWS), :], sem)
+        copy.start()
+        copy.wait()
 
 
 def body(tracer, source, offset, fraction, cutoffs):
@@ -284,7 +285,7 @@
         west = moved(tracer, lambda a, b: (a, b + 1))
         east = moved(tracer, lambda a, b: (a, b - 1))
 
-    def filter_band():
+    with jax.named_scope("pack_polar_band"):
         packed = call(
             pack_kernel,
             jax.ShapeDtypeStruct((NBLK, 4, PROWS, BLK), F32),
@@ -300,24 +301,30 @@
             60,
             1_000_000,
         )(source.reshape(1, rows), tracer, offset, fraction)
+
+    def filter_band():
         band = lax.all_to_all(packed, "lon", 0, 0)
-        kappa = jnp.where(lat == 0, cutoffs[0], cutoffs[1]).astype(F32)
-        k1 = jnp.arange(NBLK, dtype=jnp.int32)
-        k2 = jnp.arange(BLK, dtype=jnp.int32)
-        wave = k1[:, None, None] + NBLK * k2[None, None, :]
-        wave = jnp.minimum(wave, NLON - wave)
-        inside = (wave >= 1) & (wave < NLON // 2)
-        ratio = kappa[None, :, None] / jnp.maximum(wave, 1).astype(F32)
-        damping = jnp.where(inside, jnp.maximum(1.0 - ratio, 0.0), 0.0) * (1.0 / NLON)
+        tables = fourier_tables()
+        damping = jax.ShapeDtypeStruct((HALF * PROWS, BLK), F32)
+        held = [jax.ShapeDtypeStruct(table.shape, table.dtype) for table in tables]
+        prepared = call(
+            prepare_kernel,
+            (damping, *held),
+            [smem] + [vmem] * 4,
+            (vmem,) * 5,
+            [],
+            16,
+            1_000_000_000,
+        )(cutoffs, *tables)
         return call(
             polar_kernel,
             jax.ShapeDtypeStruct((NBLK, 2, PROWS, BLK), F32),
-            [vmem] * 9,
+            [vmem] * 6,
             vmem,
             [],
             16,
             400_000_000,
-        )(band, damping.reshape(NBLK * PROWS, BLK), *fourier_tables())
+        )(band, *prepared)
 
     with jax.named_scope("polar_rows"):
         filtered = lax.cond(
@@ -333,31 +340,24 @@
             west, tracer, east
         )
         other = moved(to_other, lambda a, b: (a + (1 if a % 2 else -1), b))
+        to_pair = call(border_kernel, border, [vmem] * 3 + [anyplace], vmem, [], 16, 1_000_000)(
+            west, tracer, east, other
+        )
+        pair = moved(to_pair, lambda a, b: (a + (-1 if a % 2 else 1), b))
 
     with jax.named_scope("other_rows"):
         row = blocks // NBLK - lat * rows
         column = jnp.clip(jnp.mod(blocks % NBLK - lon + 1, NBLK), 0, 2)
         place = jnp.stack([column, row])
-        inner_done, to_pair = call(
+        done = call(
             rows_kernel,
-            (field, border),
-            [smem] + [vmem] * 6,
-            (vmem, vmem),
+            field,
+            [smem] + [vmem] * 7,
+            vmem,
             [pltpu.VMEM((4, rows, BLK), F32)],
             16,
             3_000_000_000,
-        )(place, offset, fraction, west, tracer, east, other)
-        pair = moved(to_pair, lambda a, b: (a + (-1 if a % 2 else 1), b))
-        done = call(
-            edge_kernel,
-            field,
-            [smem] + [vmem] * 7,
-            vmem,
-            [],
-            16,
-            1_000_000,
-            input_output_aliases={7: 0},
-        )(place, offset, fraction, west, tracer, east, pair, inner_done)
+        )(place, offset, fraction, west, tracer, east, other, pair)
 
     with jax.named_scope("merge"):
         return call(
@@ -365,9 +365,10 @@
             field,
             [anyplace, anyplace],
             anyplace,
-            [dma((3,))],
+            [dma],
             4,
             1_000_000,
+            input_output_aliases={0: 0},
         )(done, polar)
 
 

time: 41.8 us -> 41.3 us (0.988)
  local copies, waits for them, and re-layouts: 0.83 us -> 2.75 us
  waiting for transfers between devices: 12.6 us -> 11 us
  Pallas kernels: 9.2 us -> 8.47 us
    cond x14 -> x8, local copies, waits for them, and re-layouts: 0.04 us -> 2.72 us
    all_to_all x1, waiting for transfers between devices: 9.77 us -> 7.26 us  [filter_band(): band = lax.all_to_all(packed, 'lon', 0, 0)]
    pallas_call x1, Pallas kernels: 1.18 us -> 0.1 us  [body(): call(border_kernel, border, [vmem] * 3, vmem, [], 16, 1000000)]
    all_to_all x1, waiting for transfers between devices: 1.49 us -> 2.44 us  [body(): polar = lax.all_to_all(filtered, 'lon', 0, 0).reshape(channels, PROWS, BLK)]
    unnamed x10, local copies, waits for them, and re-layouts: 0.71 us -> 0.03 us
    pallas_call x4 -> x5, Pallas kernels: 5.62 us -> 6.23 us  [the longest x1 3.17 us: body(): call(rows_kernel, field, [smem] + [vmem] * 7, vmem, [pltpu.VMEM((4, rows,...]
  transfers between devices with their start and end apart: 6 -> 6, of which waited for: 3 -> 3; matrix products, arithmetic and copies ran while one was open for 1% -> 0% of each run, Pallas kernels for 20% -> 19%
where the time goes in v3:
time: 41.3 us; the launch traced here: 40.9 us
  starting transfers between devices  18.5 us (45%)
  waiting for transfers between devices  11 us (27%)
  Pallas kernels  8.47 us (21%)
  local copies, waits for them, and re-layouts  2.75 us (7%)
    all_to_all x1, starting transfers between devices, filter_band(): band = lax.all_to_all(packed, 'lon', 0, 0)  11 us
    all_to_all x1, waiting for transfers between devices, filter_band(): band = lax.all_to_all(packed, 'lon', 0, 0)  7.26 us
    all_to_all x1, starting transfers between devices, body(): polar = lax.all_to_all(filtered, 'lon', 0, 0).reshape(channels, PROWS, BLK)  4.75 us
    pallas_call x1, Pallas kernels, body(): call(rows_kernel, field, [smem] + [vmem] * 7, vmem, [pltpu.VMEM((4, rows,...  3.17 us
    ppermute x4, starting transfers between devices, moved(): return lax.ppermute(values, ('lat', 'lon'), pairs)  2.79 us
    cond x8, local copies, waits for them, and re-layouts  2.72 us
    all_to_all x1, waiting for transfers between devices, body(): polar = lax.all_to_all(filtered, 'lon', 0, 0).reshape(channels, PROWS, BLK)  2.44 us
    pallas_call x1, Pallas kernels, filter_band(): call(polar_kernel, jax.ShapeDtypeStruct((NBLK, 2, PROWS, BLK), F32), [vme...  2.13 us
  transfers between devices with their start and end apart: 6, of which 3 were waited for; matrix products, arithmetic and copies ran while one was open for 0% of the time, Pallas kernels for 19%

profile of v3, /device:TPU:32, one launch (start us, length us, event | category | flops | bytes accessed | tf_op | source)
XLA Modules:
  0.0 40.9 jit_solution(10368467286113809977)
XLA Ops:
  0.0 1.9 %collective-permute-start = (f32[32,32,128]{2,1,0:T(8,128)}, f32[32,32,128]{2,1,0:T(8,128)S(1)}, u32[]{:S(2)}, u32[]{:S(2)}) collective-permute-start(f32[32,32,128]{2,1,0:T(8,128)} %tracer.1), channel_id=1, source_target_pairs={{0,1},{1,2},{2,3},{3,4},{4,5},{5,6},{6,7},{7,8},{8,9},{9,10},{10,1... | collective-permute-start | bytes 1572872 | tf_op jit(solution)/shard_map/lon_neighbours/ppermute | solution.py:281
  1.9 0.1 collective-permute-start.1
  2.0 1.7 %pack_polar_band.1 = f32[16,4,8,128]{3,2,1,0:T(8,128)} custom-call(s32[1,32]{1,0:T(1,128)} %bitcast.9, f32[32,32,128]{2,1,0:T(8,128)} %tracer.1, s32[32,128]{1,0:T(8,128)} %offset.3, f32[32,128]{1,0:T(8,128)} %fraction.3), custom_call_target="tpu_custom_call" | custom-call | flops 1000000 | bytes 1048576 | tf_op jit(solution)/shard_map/pack_polar_band/pallas_call | solution.py:289
  3.7 0.0 copy-done.8
  3.7 0.0 copy-start
  3.7 23.7 %conditional.1 = (f32[16,2,8,128]{3,2,1,0:T(8,128)}) conditional(s32[]{:T(128)} %convert_element_type.3, () %tuple.11, (f32[16,4,8,128]{3,2,1,0:T(8,128)}, s32[2,8]{1,0:T(2,128)S(1)}, (), (), (), /*index=5*/()) %tuple.26), branch_computations={%region_0.0_spmd, %region_1.0_spmd} | conditional | flops 1400000000 | bytes 4817048 | solution.py:330
  3.8 0.0 copy-start.4
  3.8 11.0 %all-to-all-start = ((f32[16,4,8,128]{3,2,1,0:T(8,128)}), f32[16,4,8,128]{3,2,1,0:T(8,128)S(1)}, u32[]{:S(2)}, u32[]{:S(2)}) async-start(f32[16,4,8,128]{3,2,1,0:T(8,128)} %get-tuple-element.20), calls=%async_computation | async-start | bytes 524288 | tf_op jit(solution)/shard_map/polar_rows/cond/branch_1_fun/all_to_all | solution.py:306
  14.7 0.0 copy-done.4
  14.7 0.0 copy-start.3
  14.7 0.9 %copy-done.3 = bf16[2,256,256]{2,1,0:T(8,128)(2,1)S(1)} copy-done((bf16[2,256,256]{2,1,0:T(8,128)(2,1)S(1)}, bf16[2,256,256]{2,1,0:T(8,128)(2,1)}, u32[]{:S(2)}) %copy-start.3) | copy-done | bytes 262168 | tf_op jit(solution)/shard_map/polar_rows/cond
  15.7 0.9 %copy-done.5 = bf16[2,144,128]{2,1,0:T(8,128)(2,1)S(1)} copy-done((bf16[2,144,128]{2,1,0:T(8,128)(2,1)S(1)}, bf16[2,144,128]{2,1,0:T(8,128)(2,1)}, u32[]{:S(2)}) %copy-start.5) | copy-done | bytes 73752 | tf_op jit(solution)/shard_map/polar_rows/cond
  16.6 0.9 %copy-done.6 = f32[2,72,128]{2,1,0:T(8,128)S(1)} copy-done((f32[2,72,128]{2,1,0:T(8,128)S(1)}, f32[2,72,128]{2,1,0:T(8,128)}, u32[]{:S(2)}) %copy-start.6) | copy-done | bytes 73752 | tf_op jit(solution)/shard_map/polar_rows/cond
  17.5 0.6 %branch_1_fun.2 = (f32[72,128]{1,0:T(8,128)S(1)}, bf16[2,144,128]{2,1,0:T(8,128)(2,1)S(1)}, bf16[2,128,144]{2,1,0:T(8,128)(2,1)S(1)}, bf16[2,256,256]{2,1,0:T(8,128)(2,1)S(1)}, f32[2,72,128]{2,1,0:T(8,128)S(1)}) custom-call(s32[2,8]{1,0:T(2,128)S(1)} %get-tuple-element.36.cutoffs, bf16[2,144,128]{2,1,0:T(8,128)(2,1)S(1)} %copy-done.5, ...), custom_call_target="tpu_custom_call" | custom-call | flops 1000000000 | bytes 1048576 | tf_op jit(solution)/shard_map/polar_rows/cond/branch_1_fun/pallas_call | solution.py:310
  18.1 7.3 %all-to-all-done.band = f32[16,4,8,128]{3,2,1,0:T(8,128)S(1)} async-done(((f32[16,4,8,128]{3,2,1,0:T(8,128)}), f32[16,4,8,128]{3,2,1,0:T(8,128)S(1)}, u32[]{:S(2)}, u32[]{:S(2)}) %all-to-all-start) | async-done | bytes 262176 | tf_op jit(solution)/shard_map/polar_rows/cond/branch_1_fun/all_to_all | solution.py:306
  25.3 2.1 %branch_1_fun.3 = f32[16,2,8,128]{3,2,1,0:T(8,128)} custom-call(f32[16,4,8,128]{3,2,1,0:T(8,128)S(1)} %all-to-all-done.band, f32[72,128]{1,0:T(8,128)S(1)} %get-tuple-element.26.weights, bf16[2,144,128]{2,1,0:T(8,128)(2,1)S(1)} %get-tuple-element.27.blocks, bf16[2,128,144]{2,1,0:T(8,128)(2,1)S(1)} %get-tuple-element.28.back, ...), custom_call_target="tpu_custom_call" | custom-call | flops 400000000 | bytes 1048576 | tf_op jit(solution)/shard_map/polar_rows/cond/branch_1_fun/pallas_call | solution.py:319
  27.5 4.7 %all-to-all-start.1 = ((f32[16,2,8,128]{3,2,1,0:T(8,128)}), f32[16,2,8,128]{3,2,1,0:T(8,128)S(1)}, u32[]{:S(2)}, u32[]{:S(2)}) async-start(f32[16,2,8,128]{3,2,1,0:T(8,128)} %get-tuple-element.43), calls=%async_computation.1 | async-start | bytes 262144 | tf_op jit(solution)/shard_map/polar_rows/all_to_all | solution.py:335
  32.2 0.0 collective-permute-done.west
  32.2 0.0 collective-permute-done.1.east
  32.3 0.0 copy-done
  32.3 0.1 borders.2
  32.4 0.7 %collective-permute-start.2 = (f32[3,2,32,128]{3,2,1,0:T(8,128)S(1)}, f32[3,2,32,128]{3,2,1,0:T(8,128)S(1)}, u32[]{:S(2)}, u32[]{:S(2)}) collective-permute-start(f32[3,2,32,128]{3,2,1,0:T(8,128)S(1)} %borders.2), channel_id=1, source_target_pairs={{16,32},{17,33},{18,34},{19,35},{20,36},{21,37},{22,38},{23,39},{2... | collective-permute-start | bytes 294920 | tf_op jit(solution)/shard_map/borders/ppermute | solution.py:281
  33.1 0.0 copy-start.1
  33.1 0.0 copy-start.2
  33.1 0.0 collective-permute-done.2.refs_0_.other
  33.1 0.1 borders.3
  33.2 0.1 collective-permute-start.3
  33.3 1.3 %collective-permute-done.3.pair = f32[3,2,32,128]{3,2,1,0:T(8,128)S(1)} collective-permute-done((f32[3,2,32,128]{3,2,1,0:T(8,128)S(1)}, f32[3,2,32,128]{3,2,1,0:T(8,128)S(1)}, u32[]{:S(2)}, u32[]{:S(2)}) %collective-permute-start.3) | collective-permute-done | bytes 98336 | tf_op jit(solution)/shard_map/borders/ppermute | solution.py:281
  34.6 0.0 copy-done.1
  34.6 3.2 %other_rows.1.rows_done = f32[32,32,128]{2,1,0:T(8,128)} custom-call(s32[2,32]{1,0:T(2,128)S(1)} %pad_add_fusion.place, s32[32,128]{1,0:T(8,128)S(1)} %copy-done.1, f32[32,128]{1,0:T(8,128)S(1)} %copy-done.2, f32[32,32,128]{2,1,0:T(8,128)S(1)} %collective-permute-done.west, f32[32,32,128]{2,1,0:T(8,128)S(1)} %copy-done, ...), custom_call_target="tpu_custom_call" | custom-call | flops 3000000000 | bytes 1048576 | tf_op jit(solution)/shard_map/other_rows/pallas_call | solution.py:352
  37.8 2.4 %all-to-all-done.1 = f32[16,2,8,128]{3,2,1,0:T(8,128)S(1)} async-done(((f32[16,2,8,128]{3,2,1,0:T(8,128)}), f32[16,2,8,128]{3,2,1,0:T(8,128)S(1)}, u32[]{:S(2)}, u32[]{:S(2)}) %all-to-all-start.1) | async-done | bytes 131104 | tf_op jit(solution)/shard_map/polar_rows/all_to_all | solution.py:335
  40.2 0.7 %merge.1 = f32[32,32,128]{2,1,0:T(8,128)} custom-call(f32[32,32,128]{2,1,0:T(8,128)} %other_rows.1.rows_done, f32[32,8,128]{2,1,0:T(8,128)S(1)} %bitcast.8), custom_call_target="tpu_custom_call", output_to_operand_aliasing={{}: (0, {})} | custom-call | flops 1000000 | bytes 1048576 | tf_op jit(solution)/shard_map/merge/pallas_call | solution.py:363
  (8 shorter events, 0.0 us)
Async XLA Ops:
  0.0 32.2 %collective-permute-start = (f32[32,32,128]{2,1,0:T(8,128)}, f32[32,32,128]{2,1,0:T(8,128)S(1)}, u32[]{:S(2)}, u32[]{:S(2)}) collective-permute-start(f32[32,32,128]{2,1,0:T(8,128)} %tracer.1), channel_id=1, source_target_pairs={{0,1},{1,2},{2,3},{3,4},{4,5},{5,6},{6,7},{7,8},{8,9},{9,10},{10,1... | collective-permute-start | bytes 1572872 | tf_op jit(solution)/shard_map/lon_neighbours/ppermute | solution.py:281
  1.9 30.3 %collective-permute-start.1 = (f32[32,32,128]{2,1,0:T(8,128)}, f32[32,32,128]{2,1,0:T(8,128)S(1)}, u32[]{:S(2)}, u32[]{:S(2)}) collective-permute-start(f32[32,32,128]{2,1,0:T(8,128)} %tracer.1), channel_id=1, source_target_pairs={{0,15},{1,0},{2,1},{3,2},{4,3},{5,4},{6,5},{7,6},{8,7},{9,8},{10,9... | collective-permute-start | bytes 1572872 | tf_op jit(solution)/shard_map/lon_neighbours/ppermute | solution.py:281
  2.0 1.7 %copy-start.8 = (s32[2,8]{1,0:T(2,128)S(1)}, s32[2,8]{1,0:T(2,128)}, u32[]{:S(2)}) copy-start(s32[2,8]{1,0:T(2,128)} %param.15) | copy-start | bytes 196
  3.7 28.5 %copy-start = (f32[32,32,128]{2,1,0:T(8,128)S(1)}, f32[32,32,128]{2,1,0:T(8,128)}, u32[]{:S(2)}) copy-start(f32[32,32,128]{2,1,0:T(8,128)} %tracer.1) | copy-start | bytes 1572868
  3.8 11.0 %copy-start.4 = (bf16[2,128,144]{2,1,0:T(8,128)(2,1)S(1)}, bf16[2,128,144]{2,1,0:T(8,128)(2,1)}, u32[]{:S(2)}) copy-start(bf16[2,128,144]{2,1,0:T(8,128)(2,1)} %constant.58.clone.1.refs_1_) | copy-start | bytes 221188 | tf_op jit(solution)/shard_map/polar_rows/cond
  3.8 21.6 %all-to-all-start = ((f32[16,4,8,128]{3,2,1,0:T(8,128)}), f32[16,4,8,128]{3,2,1,0:T(8,128)S(1)}, u32[]{:S(2)}, u32[]{:S(2)}) async-start(f32[16,4,8,128]{3,2,1,0:T(8,128)} %get-tuple-element.20), calls=%async_computation | async-start | bytes 524288 | tf_op jit(solution)/shard_map/polar_rows/cond/branch_1_fun/all_to_all | solution.py:306
  14.7 1.0 %copy-start.3 = (bf16[2,256,256]{2,1,0:T(8,128)(2,1)S(1)}, bf16[2,256,256]{2,1,0:T(8,128)(2,1)}, u32[]{:S(2)}) copy-start(bf16[2,256,256]{2,1,0:T(8,128)(2,1)} %constant.59.clone.1.refs_2_) | copy-start | bytes 786436 | tf_op jit(solution)/shard_map/polar_rows/cond
  15.7 0.9 %copy-start.5 = (bf16[2,144,128]{2,1,0:T(8,128)(2,1)S(1)}, bf16[2,144,128]{2,1,0:T(8,128)(2,1)}, u32[]{:S(2)}) copy-start(bf16[2,144,128]{2,1,0:T(8,128)(2,1)} %constant.57.clone.1.refs_0_) | copy-start | bytes 221188 | tf_op jit(solution)/shard_map/polar_rows/cond
  16.6 0.9 %copy-start.6 = (f32[2,72,128]{2,1,0:T(8,128)S(1)}, f32[2,72,128]{2,1,0:T(8,128)}, u32[]{:S(2)}) copy-start(f32[2,72,128]{2,1,0:T(8,128)} %constant.60.clone.1.refs_3_) | copy-start | bytes 221188 | tf_op jit(solution)/shard_map/polar_rows/cond
  27.5 12.8 %all-to-all-start.1 = ((f32[16,2,8,128]{3,2,1,0:T(8,128)}), f32[16,2,8,128]{3,2,1,0:T(8,128)S(1)}, u32[]{:S(2)}, u32[]{:S(2)}) async-start(f32[16,2,8,128]{3,2,1,0:T(8,128)} %get-tuple-element.43), calls=%async_computation.1 | async-start | bytes 262144 | tf_op jit(solution)/shard_map/polar_rows/all_to_all | solution.py:335
  32.2 0.8 %copy-start.7 = (s32[32,1]{0,1:T(1,128)S(1)}, s32[32,1]{0,1:T(1,128)}, u32[]{:S(2)}) copy-start(s32[32,1]{0,1:T(1,128)} %param.12) | copy-start | bytes 388
  32.4 0.7 %collective-permute-start.2 = (f32[3,2,32,128]{3,2,1,0:T(8,128)S(1)}, f32[3,2,32,128]{3,2,1,0:T(8,128)S(1)}, u32[]{:S(2)}, u32[]{:S(2)}) collective-permute-start(f32[3,2,32,128]{3,2,1,0:T(8,128)S(1)} %borders.2), channel_id=1, source_target_pairs={{16,32},{17,33},{18,34},{19,35},{20,36},{21,37},{22,38},{23,39},{2... | collective-permute-start | bytes 294920 | tf_op jit(solution)/shard_map/borders/ppermute | solution.py:281
  33.1 1.5 %copy-start.1 = (s32[32,128]{1,0:T(8,128)S(1)}, s32[32,128]{1,0:T(8,128)}, u32[]{:S(2)}) copy-start(s32[32,128]{1,0:T(8,128)} %offset.3) | copy-start | bytes 49156
  33.1 1.5 %copy-start.2 = (f32[32,128]{1,0:T(8,128)S(1)}, f32[32,128]{1,0:T(8,128)}, u32[]{:S(2)}) copy-start(f32[32,128]{1,0:T(8,128)} %fraction.3) | copy-start | bytes 49156
  33.2 1.4 %collective-permute-start.3 = (f32[3,2,32,128]{3,2,1,0:T(8,128)S(1)}, f32[3,2,32,128]{3,2,1,0:T(8,128)S(1)}, u32[]{:S(2)}, u32[]{:S(2)}) collective-permute-start(f32[3,2,32,128]{3,2,1,0:T(8,128)S(1)} %borders.3), channel_id=1, source_target_pairs={{0,16},{1,17},{2,18},{3,19},{4,20},{5,21},{6,22},{7,23},{8,24},{9,... | collective-permute-start | bytes 294920 | tf_op jit(solution)/shard_map/borders/ppermute | solution.py:281

commit v4 on v3

--- a/solution.py
+++ b/solution.py
@@ -246,6 +246,14 @@
         copy.wait()
 
 
+def return_groups(lat_count):
+    last = lat_count - 1
+    planes = [b + half for b in range(NBLK // 2) for half in (0, NBLK // 2)]
+    others = [a * NBLK + b for b in planes for a in range(1, last)]
+    ends = [[a * NBLK + b for b in range(NBLK)] for a in (0, last)]
+    return ends + [others[n : n + NBLK] for n in range(0, len(others), NBLK)]
+
+
 def body(tracer, source, offset, fraction, cutoffs):
     channels, rows, cells = tracer.shape
     lat_count = lax.axis_size("lat")
@@ -332,7 +340,9 @@
             filter_band,
             lambda: jnp.zeros((NBLK, 2, PROWS, BLK), F32),
         )
-        polar = lax.all_to_all(filtered, "lon", 0, 0).reshape(channels, PROWS, BLK)
+        polar = lax.all_to_all(
+            filtered, ("lat", "lon"), 0, 0, axis_index_groups=return_groups(lat_count)
+        ).reshape(channels, PROWS, BLK)
 
     with jax.named_scope("borders"):
         border = jax.ShapeDtypeStruct((3, HL, channels, cells), F32)

time: 41.3 us -> 39.8 us (0.964)
  waiting for transfers between devices: 11 us -> 9.34 us
    all_to_all x1, waiting for transfers between devices: 7.26 us -> 5.62 us  [filter_band(): band = lax.all_to_all(packed, 'lon', 0, 0)]
  transfers between devices with their start and end apart: 6 -> 6, of which waited for: 3 -> 3; matrix products, arithmetic and copies ran while one was open for 0% -> 0% of each run, Pallas kernels for 19% -> 20%
where the time goes in v4:
time: 39.8 us; the launch traced here: 39.4 us
  starting transfers between devices  18.6 us (47%)
  waiting for transfers between devices  9.34 us (23%)
  Pallas kernels  8.47 us (21%)
  local copies, waits for them, and re-layouts  2.75 us (7%)
    all_to_all x1, starting transfers between devices, filter_band(): band = lax.all_to_all(packed, 'lon', 0, 0)  11 us
    all_to_all x1, waiting for transfers between devices, filter_band(): band = lax.all_to_all(packed, 'lon', 0, 0)  5.62 us
    all_to_all x1, starting transfers between devices, body(): lax.all_to_all(filtered, ('lat', 'lon'), 0, 0, axis_index_groups=return_g...  4.86 us
    pallas_call x1, Pallas kernels, body(): call(rows_kernel, field, [smem] + [vmem] * 7, vmem, [pltpu.VMEM((4, rows,...  3.17 us
    ppermute x4, starting transfers between devices, moved(): return lax.ppermute(values, ('lat', 'lon'), pairs)  2.79 us
    cond x8, local copies, waits for them, and re-layouts  2.72 us
    all_to_all x1, waiting for transfers between devices, body(): lax.all_to_all(filtered, ('lat', 'lon'), 0, 0, axis_index_groups=return_g...  2.44 us
    pallas_call x1, Pallas kernels, filter_band(): call(polar_kernel, jax.ShapeDtypeStruct((NBLK, 2, PROWS, BLK), F32), [vme...  2.13 us
  transfers between devices with their start and end apart: 6, of which 3 were waited for; matrix products, arithmetic and copies ran while one was open for 0% of the time, Pallas kernels for 20%

profile of v4, /device:TPU:32, one launch (start us, length us, event | category | flops | bytes accessed | tf_op | source)
XLA Modules:
  0.0 39.4 jit_solution(14064774864640344568)
XLA Ops:
  0.0 1.9 %collective-permute-start = (f32[32,32,128]{2,1,0:T(8,128)}, f32[32,32,128]{2,1,0:T(8,128)S(1)}, u32[]{:S(2)}, u32[]{:S(2)}) collective-permute-start(f32[32,32,128]{2,1,0:T(8,128)} %tracer.1), channel_id=1, source_target_pairs={{0,1},{1,2},{2,3},{3,4},{4,5},{5,6},{6,7},{7,8},{8,9},{9,10},{10,1... | collective-permute-start | bytes 1572872 | tf_op jit(solution)/shard_map/lon_neighbours/ppermute | solution.py:289
  1.9 0.1 collective-permute-start.1
  2.0 1.7 %pack_polar_band.1 = f32[16,4,8,128]{3,2,1,0:T(8,128)} custom-call(s32[1,32]{1,0:T(1,128)} %bitcast.9, f32[32,32,128]{2,1,0:T(8,128)} %tracer.1, s32[32,128]{1,0:T(8,128)} %offset.3, f32[32,128]{1,0:T(8,128)} %fraction.3), custom_call_target="tpu_custom_call" | custom-call | flops 1000000 | bytes 1048576 | tf_op jit(solution)/shard_map/pack_polar_band/pallas_call | solution.py:297
  3.7 0.0 copy-done.8
  3.7 0.0 copy-start
  3.7 22.1 %conditional.1 = (f32[16,2,8,128]{3,2,1,0:T(8,128)}) conditional(s32[]{:T(128)} %convert_element_type.3, () %tuple.11, (f32[16,4,8,128]{3,2,1,0:T(8,128)}, s32[2,8]{1,0:T(2,128)S(1)}, (), (), (), /*index=5*/()) %tuple.26), branch_computations={%region_0.0_spmd, %region_1.0_spmd} | conditional | flops 1400000000 | bytes 4817048 | solution.py:338
  3.8 0.0 copy-start.4
  3.8 11.0 %all-to-all-start = ((f32[16,4,8,128]{3,2,1,0:T(8,128)}), f32[16,4,8,128]{3,2,1,0:T(8,128)S(1)}, u32[]{:S(2)}, u32[]{:S(2)}) async-start(f32[16,4,8,128]{3,2,1,0:T(8,128)} %get-tuple-element.20), calls=%async_computation | async-start | bytes 524288 | tf_op jit(solution)/shard_map/polar_rows/cond/branch_1_fun/all_to_all | solution.py:314
  14.7 0.0 copy-done.4
  14.7 0.0 copy-start.3
  14.7 0.9 %copy-done.3 = bf16[2,256,256]{2,1,0:T(8,128)(2,1)S(1)} copy-done((bf16[2,256,256]{2,1,0:T(8,128)(2,1)S(1)}, bf16[2,256,256]{2,1,0:T(8,128)(2,1)}, u32[]{:S(2)}) %copy-start.3) | copy-done | bytes 262168 | tf_op jit(solution)/shard_map/polar_rows/cond
  15.7 0.9 %copy-done.5 = bf16[2,144,128]{2,1,0:T(8,128)(2,1)S(1)} copy-done((bf16[2,144,128]{2,1,0:T(8,128)(2,1)S(1)}, bf16[2,144,128]{2,1,0:T(8,128)(2,1)}, u32[]{:S(2)}) %copy-start.5) | copy-done | bytes 73752 | tf_op jit(solution)/shard_map/polar_rows/cond
  16.6 0.9 %copy-done.6 = f32[2,72,128]{2,1,0:T(8,128)S(1)} copy-done((f32[2,72,128]{2,1,0:T(8,128)S(1)}, f32[2,72,128]{2,1,0:T(8,128)}, u32[]{:S(2)}) %copy-start.6) | copy-done | bytes 73752 | tf_op jit(solution)/shard_map/polar_rows/cond
  17.5 0.6 %branch_1_fun.2 = (f32[72,128]{1,0:T(8,128)S(1)}, bf16[2,144,128]{2,1,0:T(8,128)(2,1)S(1)}, bf16[2,128,144]{2,1,0:T(8,128)(2,1)S(1)}, bf16[2,256,256]{2,1,0:T(8,128)(2,1)S(1)}, f32[2,72,128]{2,1,0:T(8,128)S(1)}) custom-call(s32[2,8]{1,0:T(2,128)S(1)} %get-tuple-element.36.cutoffs, bf16[2,144,128]{2,1,0:T(8,128)(2,1)S(1)} %copy-done.5, ...), custom_call_target="tpu_custom_call" | custom-call | flops 1000000000 | bytes 1048576 | tf_op jit(solution)/shard_map/polar_rows/cond/branch_1_fun/pallas_call | solution.py:318
  18.1 5.6 %all-to-all-done.band = f32[16,4,8,128]{3,2,1,0:T(8,128)S(1)} async-done(((f32[16,4,8,128]{3,2,1,0:T(8,128)}), f32[16,4,8,128]{3,2,1,0:T(8,128)S(1)}, u32[]{:S(2)}, u32[]{:S(2)}) %all-to-all-start) | async-done | bytes 262176 | tf_op jit(solution)/shard_map/polar_rows/cond/branch_1_fun/all_to_all | solution.py:314
  23.7 2.1 %branch_1_fun.3 = f32[16,2,8,128]{3,2,1,0:T(8,128)} custom-call(f32[16,4,8,128]{3,2,1,0:T(8,128)S(1)} %all-to-all-done.band, f32[72,128]{1,0:T(8,128)S(1)} %get-tuple-element.26.weights, bf16[2,144,128]{2,1,0:T(8,128)(2,1)S(1)} %get-tuple-element.27.blocks, bf16[2,128,144]{2,1,0:T(8,128)(2,1)S(1)} %get-tuple-element.28.back, ...), custom_call_target="tpu_custom_call" | custom-call | flops 400000000 | bytes 1048576 | tf_op jit(solution)/shard_map/polar_rows/cond/branch_1_fun/pallas_call | solution.py:327
  25.8 4.9 %all-to-all-start.1 = ((f32[16,2,8,128]{3,2,1,0:T(8,128)}), f32[16,2,8,128]{3,2,1,0:T(8,128)S(1)}, u32[]{:S(2)}, u32[]{:S(2)}) async-start(f32[16,2,8,128]{3,2,1,0:T(8,128)} %get-tuple-element.43), calls=%async_computation.1 | async-start | bytes 262144 | tf_op jit(solution)/shard_map/polar_rows/all_to_all | solution.py:343
  30.7 0.0 collective-permute-done.west
  30.7 0.0 collective-permute-done.1.east
  30.7 0.0 copy-done
  30.7 0.1 borders.2
  30.8 0.7 %collective-permute-start.2 = (f32[3,2,32,128]{3,2,1,0:T(8,128)S(1)}, f32[3,2,32,128]{3,2,1,0:T(8,128)S(1)}, u32[]{:S(2)}, u32[]{:S(2)}) collective-permute-start(f32[3,2,32,128]{3,2,1,0:T(8,128)S(1)} %borders.2), channel_id=1, source_target_pairs={{16,32},{17,33},{18,34},{19,35},{20,36},{21,37},{22,38},{23,39},{2... | collective-permute-start | bytes 294920 | tf_op jit(solution)/shard_map/borders/ppermute | solution.py:289
  31.5 0.0 copy-done.7
  31.6 0.0 copy-start.1
  31.6 0.0 copy-start.2
  31.6 0.0 collective-permute-done.2.refs_0_.other
  31.6 0.1 borders.3
  31.7 0.1 collective-permute-start.3
  31.8 1.3 %collective-permute-done.3.pair = f32[3,2,32,128]{3,2,1,0:T(8,128)S(1)} collective-permute-done((f32[3,2,32,128]{3,2,1,0:T(8,128)S(1)}, f32[3,2,32,128]{3,2,1,0:T(8,128)S(1)}, u32[]{:S(2)}, u32[]{:S(2)}) %collective-permute-start.3) | collective-permute-done | bytes 98336 | tf_op jit(solution)/shard_map/borders/ppermute | solution.py:289
  33.1 3.2 %other_rows.1.rows_done = f32[32,32,128]{2,1,0:T(8,128)} custom-call(s32[2,32]{1,0:T(2,128)S(1)} %pad_add_fusion.place, s32[32,128]{1,0:T(8,128)S(1)} %copy-done.1, f32[32,128]{1,0:T(8,128)S(1)} %copy-done.2, f32[32,32,128]{2,1,0:T(8,128)S(1)} %collective-permute-done.west, f32[32,32,128]{2,1,0:T(8,128)S(1)} %copy-done, ...), custom_call_target="tpu_custom_call" | custom-call | flops 3000000000 | bytes 1048576 | tf_op jit(solution)/shard_map/other_rows/pallas_call | solution.py:362
  36.3 2.4 %all-to-all-done.1 = f32[16,2,8,128]{3,2,1,0:T(8,128)S(1)} async-done(((f32[16,2,8,128]{3,2,1,0:T(8,128)}), f32[16,2,8,128]{3,2,1,0:T(8,128)S(1)}, u32[]{:S(2)}, u32[]{:S(2)}) %all-to-all-start.1) | async-done | bytes 131104 | tf_op jit(solution)/shard_map/polar_rows/all_to_all | solution.py:343
  38.7 0.7 %merge.1 = f32[32,32,128]{2,1,0:T(8,128)} custom-call(f32[32,32,128]{2,1,0:T(8,128)} %other_rows.1.rows_done, f32[32,8,128]{2,1,0:T(8,128)S(1)} %bitcast.8), custom_call_target="tpu_custom_call", output_to_operand_aliasing={{}: (0, {})} | custom-call | flops 1000000 | bytes 1048576 | tf_op jit(solution)/shard_map/merge/pallas_call | solution.py:373
  (8 shorter events, 0.0 us)
Async XLA Ops:
  0.0 30.7 %collective-permute-start = (f32[32,32,128]{2,1,0:T(8,128)}, f32[32,32,128]{2,1,0:T(8,128)S(1)}, u32[]{:S(2)}, u32[]{:S(2)}) collective-permute-start(f32[32,32,128]{2,1,0:T(8,128)} %tracer.1), channel_id=1, source_target_pairs={{0,1},{1,2},{2,3},{3,4},{4,5},{5,6},{6,7},{7,8},{8,9},{9,10},{10,1... | collective-permute-start | bytes 1572872 | tf_op jit(solution)/shard_map/lon_neighbours/ppermute | solution.py:289
  1.9 28.8 %collective-permute-start.1 = (f32[32,32,128]{2,1,0:T(8,128)}, f32[32,32,128]{2,1,0:T(8,128)S(1)}, u32[]{:S(2)}, u32[]{:S(2)}) collective-permute-start(f32[32,32,128]{2,1,0:T(8,128)} %tracer.1), channel_id=1, source_target_pairs={{0,15},{1,0},{2,1},{3,2},{4,3},{5,4},{6,5},{7,6},{8,7},{9,8},{10,9... | collective-permute-start | bytes 1572872 | tf_op jit(solution)/shard_map/lon_neighbours/ppermute | solution.py:289
  2.0 1.7 %copy-start.8 = (s32[2,8]{1,0:T(2,128)S(1)}, s32[2,8]{1,0:T(2,128)}, u32[]{:S(2)}) copy-start(s32[2,8]{1,0:T(2,128)} %param.15) | copy-start | bytes 196
  3.7 27.0 %copy-start = (f32[32,32,128]{2,1,0:T(8,128)S(1)}, f32[32,32,128]{2,1,0:T(8,128)}, u32[]{:S(2)}) copy-start(f32[32,32,128]{2,1,0:T(8,128)} %tracer.1) | copy-start | bytes 1572868
  3.8 11.0 %copy-start.4 = (bf16[2,128,144]{2,1,0:T(8,128)(2,1)S(1)}, bf16[2,128,144]{2,1,0:T(8,128)(2,1)}, u32[]{:S(2)}) copy-start(bf16[2,128,144]{2,1,0:T(8,128)(2,1)} %constant.58.clone.1.refs_1_) | copy-start | bytes 221188 | tf_op jit(solution)/shard_map/polar_rows/cond
  3.8 19.9 %all-to-all-start = ((f32[16,4,8,128]{3,2,1,0:T(8,128)}), f32[16,4,8,128]{3,2,1,0:T(8,128)S(1)}, u32[]{:S(2)}, u32[]{:S(2)}) async-start(f32[16,4,8,128]{3,2,1,0:T(8,128)} %get-tuple-element.20), calls=%async_computation | async-start | bytes 524288 | tf_op jit(solution)/shard_map/polar_rows/cond/branch_1_fun/all_to_all | solution.py:314
  14.7 1.0 %copy-start.3 = (bf16[2,256,256]{2,1,0:T(8,128)(2,1)S(1)}, bf16[2,256,256]{2,1,0:T(8,128)(2,1)}, u32[]{:S(2)}) copy-start(bf16[2,256,256]{2,1,0:T(8,128)(2,1)} %constant.59.clone.1.refs_2_) | copy-start | bytes 786436 | tf_op jit(solution)/shard_map/polar_rows/cond
  15.7 0.9 %copy-start.5 = (bf16[2,144,128]{2,1,0:T(8,128)(2,1)S(1)}, bf16[2,144,128]{2,1,0:T(8,128)(2,1)}, u32[]{:S(2)}) copy-start(bf16[2,144,128]{2,1,0:T(8,128)(2,1)} %constant.57.clone.1.refs_0_) | copy-start | bytes 221188 | tf_op jit(solution)/shard_map/polar_rows/cond
  16.6 0.9 %copy-start.6 = (f32[2,72,128]{2,1,0:T(8,128)S(1)}, f32[2,72,128]{2,1,0:T(8,128)}, u32[]{:S(2)}) copy-start(f32[2,72,128]{2,1,0:T(8,128)} %constant.60.clone.1.refs_3_) | copy-start | bytes 221188 | tf_op jit(solution)/shard_map/polar_rows/cond
  25.8 12.9 %all-to-all-start.1 = ((f32[16,2,8,128]{3,2,1,0:T(8,128)}), f32[16,2,8,128]{3,2,1,0:T(8,128)S(1)}, u32[]{:S(2)}, u32[]{:S(2)}) async-start(f32[16,2,8,128]{3,2,1,0:T(8,128)} %get-tuple-element.43), calls=%async_computation.1 | async-start | bytes 262144 | tf_op jit(solution)/shard_map/polar_rows/all_to_all | solution.py:343
  30.7 0.8 %copy-start.7 = (s32[32,1]{0,1:T(1,128)S(1)}, s32[32,1]{0,1:T(1,128)}, u32[]{:S(2)}) copy-start(s32[32,1]{0,1:T(1,128)} %param.12) | copy-start | bytes 388
  30.8 0.7 %collective-permute-start.2 = (f32[3,2,32,128]{3,2,1,0:T(8,128)S(1)}, f32[3,2,32,128]{3,2,1,0:T(8,128)S(1)}, u32[]{:S(2)}, u32[]{:S(2)}) collective-permute-start(f32[3,2,32,128]{3,2,1,0:T(8,128)S(1)} %borders.2), channel_id=1, source_target_pairs={{16,32},{17,33},{18,34},{19,35},{20,36},{21,37},{22,38},{23,39},{2... | collective-permute-start | bytes 294920 | tf_op jit(solution)/shard_map/borders/ppermute | solution.py:289
  31.6 1.5 %copy-start.1 = (s32[32,128]{1,0:T(8,128)S(1)}, s32[32,128]{1,0:T(8,128)}, u32[]{:S(2)}) copy-start(s32[32,128]{1,0:T(8,128)} %offset.3) | copy-start | bytes 49156
  31.6 1.5 %copy-start.2 = (f32[32,128]{1,0:T(8,128)S(1)}, f32[32,128]{1,0:T(8,128)}, u32[]{:S(2)}) copy-start(f32[32,128]{1,0:T(8,128)} %fraction.3) | copy-start | bytes 49156
  31.7 1.4 %collective-permute-start.3 = (f32[3,2,32,128]{3,2,1,0:T(8,128)S(1)}, f32[3,2,32,128]{3,2,1,0:T(8,128)S(1)}, u32[]{:S(2)}, u32[]{:S(2)}) collective-permute-start(f32[3,2,32,128]{3,2,1,0:T(8,128)S(1)} %borders.3), channel_id=1, source_target_pairs={{0,16},{1,17},{2,18},{3,19},{4,20},{5,21},{6,22},{7,23},{8,24},{9,... | collective-permute-start | bytes 294920 | tf_op jit(solution)/shard_map/borders/ppermute | solution.py:289

commit v5 on v4

--- a/solution.py
+++ b/solution.py
@@ -44,9 +44,10 @@
     return jnp.minimum(jnp.maximum(interpolated, lowest_bound), upper_bound)
 
 
-def two_pieces(table):
+def three_products(table, axis):
     high = table.astype(ml_dtypes.bfloat16)
-    return np.stack([high, (table - high.astype(np.float64)).astype(ml_dtypes.bfloat16)])
+    low = (table - high.astype(np.float64)).astype(ml_dtypes.bfloat16)
+    return np.concatenate([high, high, low], axis)
 
 
 def fourier_tables():
@@ -62,16 +63,17 @@
     cells = np.block([[cosine, -sine], [sine, cosine]])
     angles = 2.0 * math.pi * np.repeat(np.outer(k1, i), PROWS, 0) / NLON
     turn = np.stack([np.cos(angles), -np.sin(angles)]).astype(np.float32)
-    return two_pieces(blocks), two_pieces(back), two_pieces(cells), turn
+    return three_products(blocks, 1), three_products(back, 1), three_products(cells, 0), turn
 
 
 def dot(left, right):
     return jnp.dot(left, right, preferred_element_type=F32)
 
 
-def split(values):
+def pieces(values, axis):
     high = values.astype(BF16)
-    return high, (values - high.astype(F32)).astype(BF16)
+    low = (values - high.astype(F32)).astype(BF16)
+    return jnp.concatenate([high, low, high], axis)
 
 
 def pack_kernel(source, tracer, offset, fraction, out, block, slab, cells, aux, sems):
@@ -125,9 +127,6 @@
 
 
 def polar_kernel(band, weights, blocks, back, cells, turn, out):
-    blocks_h, blocks_l = blocks[0], blocks[1]
-    back_h, back_l = back[0], back[1]
-    cells_h, cells_l = cells[0], cells[1]
     count = NBLK * PROWS
     half = HALF * PROWS
     anchor = band[:, 2].reshape(count, BLK).astype(jnp.int32)
@@ -139,7 +138,7 @@
     rest = own - high.astype(F32)
     middle = rest.astype(BF16)
     low = (rest - middle.astype(F32)).astype(BF16)
-    picked = dot(chosen, high) + dot(chosen, middle) + dot(chosen, low)
+    picked = dot(jnp.concatenate([chosen] * 3, 1), jnp.concatenate([high, middle, low], 0))
     cell = anchor & 127
     cubic = cubic_weights(band[:, 3].reshape(count, BLK))
     limited = [
@@ -147,29 +146,24 @@
         cubic_limited(picked[:, BLK:], cell, cubic),
     ]
     turn_r, turn_i = turn[0], turn[1]
-    high, low = split(jnp.concatenate(limited, 1))
-    first = dot(blocks_h, high) + dot(blocks_h, low) + dot(blocks_l, high)
+    first = dot(blocks[...], pieces(jnp.concatenate(limited, 1), 0))
     parts = []
     for c in range(2):
         real, imag = first[:half, c * BLK : (c + 1) * BLK], first[half:, c * BLK : (c + 1) * BLK]
         parts.append(
             jnp.concatenate([real * turn_r - imag * turn_i, real * turn_i + imag * turn_r], 1)
         )
-    high, low = split(jnp.concatenate(parts, 0))
-    spectrum = dot(high, cells_h) + dot(low, cells_h) + dot(high, cells_l)
+    spectrum = dot(pieces(jnp.concatenate(parts, 0), 1), cells[...])
     damping = jnp.concatenate([weights[...], weights[...]], 0)
     damped = jnp.concatenate([spectrum[:, BLK:] * damping, spectrum[:, :BLK] * damping], 1)
-    high, low = split(damped)
-    second = dot(high, cells_h) + dot(low, cells_h) + dot(high, cells_l)
+    second = dot(pieces(damped, 1), cells[...])
     reals, imags = [], []
     for c in range(2):
         imag, real = second[c * half : (c + 1) * half, :BLK], second[c * half : (c + 1) * half, BLK:]
         reals.append(real * turn_r + imag * turn_i)
         imags.append(imag * turn_r - real * turn_i)
-    high, low = split(
-        jnp.concatenate([jnp.concatenate(reals, 1), jnp.concatenate(imags, 1)], 0)
-    )
-    removed = dot(back_h, high) + dot(back_h, low) + dot(back_l, high)
+    both = jnp.concatenate([jnp.concatenate(reals, 1), jnp.concatenate(imags, 1)], 0)
+    removed = dot(back[...], pieces(both, 0))
     for c in range(2):
         kept = limited[c] - removed[:, c * BLK : (c + 1) * BLK]
         out[:, c] = kept.reshape(NBLK, PROWS, BLK)
@@ -208,7 +202,7 @@
     return jnp.where(outside, halo(column, beyond), own_values(columns, column, row))
 
 
-def rows_kernel(place, offset, fraction, west, own, east, other, pair, out, cubic):
+def rows_kernel(place, offset, fraction, east, own, west, other, pair, out, cubic):
     first_of_pair = lax.axis_index("lat") % 2 == 0
     channels, rows = own.shape[0], own.shape[1]
     columns = (west, own, east)
@@ -367,7 +361,7 @@
             [pltpu.VMEM((4, rows, BLK), F32)],
             16,
             3_000_000_000,
-        )(place, offset, fraction, west, tracer, east, other, pair)
+        )(place, offset, fraction, east, tracer, west, other, pair)
 
     with jax.named_scope("merge"):
         return call(

time: 39.8 us -> 39.7 us (level)
  no operation moved by 1% of the time
where the time goes in v5:
time: 39.7 us; the launch traced here: 39.3 us
  starting transfers between devices  18.6 us (47%)
  waiting for transfers between devices  9.28 us (23%)
  Pallas kernels  8.39 us (21%)
  local copies, waits for them, and re-layouts  2.8 us (7%)
    all_to_all x1, starting transfers between devices, filter_band(): band = lax.all_to_all(packed, 'lon', 0, 0)  11 us
    all_to_all x1, waiting for transfers between devices, filter_band(): band = lax.all_to_all(packed, 'lon', 0, 0)  5.56 us
    all_to_all x1, starting transfers between devices, body(): lax.all_to_all(filtered, ('lat', 'lon'), 0, 0, axis_index_groups=return_g...  4.86 us
    pallas_call x1, Pallas kernels, body(): call(rows_kernel, field, [smem] + [vmem] * 7, vmem, [pltpu.VMEM((4, rows,...  3.17 us
    ppermute x4, starting transfers between devices, moved(): return lax.ppermute(values, ('lat', 'lon'), pairs)  2.79 us
    cond x8, local copies, waits for them, and re-layouts  2.78 us
    all_to_all x1, waiting for transfers between devices, body(): lax.all_to_all(filtered, ('lat', 'lon'), 0, 0, axis_index_groups=return_g...  2.44 us
    pallas_call x1, Pallas kernels, filter_band(): call(polar_kernel, jax.ShapeDtypeStruct((NBLK, 2, PROWS, BLK), F32), [vme...  2.05 us
  transfers between devices with their start and end apart: 6, of which 3 were waited for; matrix products, arithmetic and copies ran while one was open for 0% of the time, Pallas kernels for 20%

profile of v5, /device:TPU:32, one launch (start us, length us, event | category | flops | bytes accessed | tf_op | source)
XLA Modules:
  0.0 39.3 jit_solution(14352920892059599706)
XLA Ops:
  0.0 1.9 %collective-permute-start.1 = (f32[32,32,128]{2,1,0:T(8,128)}, f32[32,32,128]{2,1,0:T(8,128)S(1)}, u32[]{:S(2)}, u32[]{:S(2)}) collective-permute-start(f32[32,32,128]{2,1,0:T(8,128)} %tracer.1), channel_id=1, source_target_pairs={{0,1},{1,2},{2,3},{3,4},{4,5},{5,6},{6,7},{7,8},{8,9},{9,10},{10,1... | collective-permute-start | bytes 1572872 | tf_op jit(solution)/shard_map/lon_neighbours/ppermute | solution.py:283
  1.9 0.1 collective-permute-start
  2.0 1.7 %pack_polar_band.1 = f32[16,4,8,128]{3,2,1,0:T(8,128)} custom-call(s32[1,32]{1,0:T(1,128)} %bitcast.9, f32[32,32,128]{2,1,0:T(8,128)} %tracer.1, s32[32,128]{1,0:T(8,128)} %offset.3, f32[32,128]{1,0:T(8,128)} %fraction.3), custom_call_target="tpu_custom_call" | custom-call | flops 1000000 | bytes 1048576 | tf_op jit(solution)/shard_map/pack_polar_band/pallas_call | solution.py:291
  3.7 0.0 copy-done.8
  3.7 0.0 copy-start
  3.7 22.0 %conditional.1 = (f32[16,2,8,128]{3,2,1,0:T(8,128)}) conditional(s32[]{:T(128)} %convert_element_type.3, () %tuple.11, (f32[16,4,8,128]{3,2,1,0:T(8,128)}, s32[2,8]{1,0:T(2,128)S(1)}, (), (), (), /*index=5*/()) %tuple.26), branch_computations={%region_0.0_spmd, %region_1.0_spmd} | conditional | flops 1400000000 | bytes 5636248 | solution.py:332
  3.8 0.0 copy-start.4
  3.8 11.0 %all-to-all-start = ((f32[16,4,8,128]{3,2,1,0:T(8,128)}), f32[16,4,8,128]{3,2,1,0:T(8,128)S(1)}, u32[]{:S(2)}, u32[]{:S(2)}) async-start(f32[16,4,8,128]{3,2,1,0:T(8,128)} %get-tuple-element.20), calls=%async_computation | async-start | bytes 524288 | tf_op jit(solution)/shard_map/polar_rows/cond/branch_1_fun/all_to_all | solution.py:308
  14.7 0.0 copy-done.4
  14.7 0.0 copy-start.3
  14.7 1.0 %copy-done.3 = bf16[768,256]{1,0:T(8,128)(2,1)S(1)} copy-done((bf16[768,256]{1,0:T(8,128)(2,1)S(1)}, bf16[768,256]{1,0:T(8,128)(2,1)}, u32[]{:S(2)}) %copy-start.3) | copy-done | bytes 393240 | tf_op jit(solution)/shard_map/polar_rows/cond
  15.7 0.9 %copy-done.5 = bf16[144,384]{1,0:T(8,128)(2,1)S(1)} copy-done((bf16[144,384]{1,0:T(8,128)(2,1)S(1)}, bf16[144,384]{1,0:T(8,128)(2,1)}, u32[]{:S(2)}) %copy-start.5) | copy-done | bytes 110616 | tf_op jit(solution)/shard_map/polar_rows/cond
  16.6 0.9 %copy-done.6 = f32[2,72,128]{2,1,0:T(8,128)S(1)} copy-done((f32[2,72,128]{2,1,0:T(8,128)S(1)}, f32[2,72,128]{2,1,0:T(8,128)}, u32[]{:S(2)}) %copy-start.6) | copy-done | bytes 73752 | tf_op jit(solution)/shard_map/polar_rows/cond
  17.5 0.6 %branch_1_fun.2 = (f32[72,128]{1,0:T(8,128)S(1)}, bf16[144,384]{1,0:T(8,128)(2,1)S(1)}, bf16[128,432]{1,0:T(8,128)(2,1)S(1)}, bf16[768,256]{1,0:T(8,128)(2,1)S(1)}, f32[2,72,128]{2,1,0:T(8,128)S(1)}) custom-call(s32[2,8]{1,0:T(2,128)S(1)} %get-tuple-element.36.cutoffs, bf16[144,384]{1,0:T(8,128)(2,1)S(1)} %copy-done.5, bf16[128,432]{1,0:T(8,128)(2,1)S(1)} %copy-done.4, ...), custom_call_target="tpu_custom_call" | custom-call | flops 1000000000 | bytes 1048576 | tf_op jit(solution)/shard_map/polar_rows/cond/branch_1_fun/pallas_call | solution.py:312
  18.1 5.6 %all-to-all-done.band = f32[16,4,8,128]{3,2,1,0:T(8,128)S(1)} async-done(((f32[16,4,8,128]{3,2,1,0:T(8,128)}), f32[16,4,8,128]{3,2,1,0:T(8,128)S(1)}, u32[]{:S(2)}, u32[]{:S(2)}) %all-to-all-start) | async-done | bytes 262176 | tf_op jit(solution)/shard_map/polar_rows/cond/branch_1_fun/all_to_all | solution.py:308
  23.7 2.0 %branch_1_fun.3 = f32[16,2,8,128]{3,2,1,0:T(8,128)} custom-call(f32[16,4,8,128]{3,2,1,0:T(8,128)S(1)} %all-to-all-done.band, f32[72,128]{1,0:T(8,128)S(1)} %get-tuple-element.26.weights, bf16[144,384]{1,0:T(8,128)(2,1)S(1)} %get-tuple-element.27.blocks, bf16[128,432]{1,0:T(8,128)(2,1)S(1)} %get-tuple-element.28.back, ...), custom_call_target="tpu_custom_call" | custom-call | flops 400000000 | bytes 1048576 | tf_op jit(solution)/shard_map/polar_rows/cond/branch_1_fun/pallas_call | solution.py:321
  25.8 4.9 %all-to-all-start.1 = ((f32[16,2,8,128]{3,2,1,0:T(8,128)}), f32[16,2,8,128]{3,2,1,0:T(8,128)S(1)}, u32[]{:S(2)}, u32[]{:S(2)}) async-start(f32[16,2,8,128]{3,2,1,0:T(8,128)} %get-tuple-element.43), calls=%async_computation.1 | async-start | bytes 262144 | tf_op jit(solution)/shard_map/polar_rows/all_to_all | solution.py:337
  30.6 0.0 collective-permute-done.1.west
  30.6 0.0 collective-permute-done.east
  30.6 0.0 copy-done
  30.6 0.1 borders.2
  30.8 0.7 %collective-permute-start.2 = (f32[3,2,32,128]{3,2,1,0:T(8,128)S(1)}, f32[3,2,32,128]{3,2,1,0:T(8,128)S(1)}, u32[]{:S(2)}, u32[]{:S(2)}) collective-permute-start(f32[3,2,32,128]{3,2,1,0:T(8,128)S(1)} %borders.2), channel_id=1, source_target_pairs={{16,32},{17,33},{18,34},{19,35},{20,36},{21,37},{22,38},{23,39},{2... | collective-permute-start | bytes 294920 | tf_op jit(solution)/shard_map/borders/ppermute | solution.py:283
  31.5 0.0 copy-start.1
  31.5 0.0 copy-start.2
  31.5 0.0 collective-permute-done.2.refs_0_.other
  31.5 0.1 borders.3
  31.6 0.1 collective-permute-start.3
  31.7 1.3 %collective-permute-done.3.pair = f32[3,2,32,128]{3,2,1,0:T(8,128)S(1)} collective-permute-done((f32[3,2,32,128]{3,2,1,0:T(8,128)S(1)}, f32[3,2,32,128]{3,2,1,0:T(8,128)S(1)}, u32[]{:S(2)}, u32[]{:S(2)}) %collective-permute-start.3) | collective-permute-done | bytes 98336 | tf_op jit(solution)/shard_map/borders/ppermute | solution.py:283
  33.0 0.0 copy-done.2
  33.0 3.2 %other_rows.1.rows_done = f32[32,32,128]{2,1,0:T(8,128)} custom-call(s32[2,32]{1,0:T(2,128)S(1)} %pad_add_fusion.place, s32[32,128]{1,0:T(8,128)S(1)} %copy-done.1, f32[32,128]{1,0:T(8,128)S(1)} %copy-done.2, f32[32,32,128]{2,1,0:T(8,128)S(1)} %collective-permute-done.east, f32[32,32,128]{2,1,0:T(8,128)S(1)} %copy-done, ...), custom_call_target="tpu_custom_call" | custom-call | flops 3000000000 | bytes 1048576 | tf_op jit(solution)/shard_map/other_rows/pallas_call | solution.py:356
  36.2 2.4 %all-to-all-done.1 = f32[16,2,8,128]{3,2,1,0:T(8,128)S(1)} async-done(((f32[16,2,8,128]{3,2,1,0:T(8,128)}), f32[16,2,8,128]{3,2,1,0:T(8,128)S(1)}, u32[]{:S(2)}, u32[]{:S(2)}) %all-to-all-start.1) | async-done | bytes 131104 | tf_op jit(solution)/shard_map/polar_rows/all_to_all | solution.py:337
  38.6 0.7 %merge.1 = f32[32,32,128]{2,1,0:T(8,128)} custom-call(f32[32,32,128]{2,1,0:T(8,128)} %other_rows.1.rows_done, f32[32,8,128]{2,1,0:T(8,128)S(1)} %bitcast.8), custom_call_target="tpu_custom_call", output_to_operand_aliasing={{}: (0, {})} | custom-call | flops 1000000 | bytes 1048576 | tf_op jit(solution)/shard_map/merge/pallas_call | solution.py:367
  (8 shorter events, 0.0 us)
Async XLA Ops:
  0.0 30.6 %collective-permute-start.1 = (f32[32,32,128]{2,1,0:T(8,128)}, f32[32,32,128]{2,1,0:T(8,128)S(1)}, u32[]{:S(2)}, u32[]{:S(2)}) collective-permute-start(f32[32,32,128]{2,1,0:T(8,128)} %tracer.1), channel_id=1, source_target_pairs={{0,1},{1,2},{2,3},{3,4},{4,5},{5,6},{6,7},{7,8},{8,9},{9,10},{10,1... | collective-permute-start | bytes 1572872 | tf_op jit(solution)/shard_map/lon_neighbours/ppermute | solution.py:283
  1.9 28.7 %collective-permute-start = (f32[32,32,128]{2,1,0:T(8,128)}, f32[32,32,128]{2,1,0:T(8,128)S(1)}, u32[]{:S(2)}, u32[]{:S(2)}) collective-permute-start(f32[32,32,128]{2,1,0:T(8,128)} %tracer.1), channel_id=1, source_target_pairs={{0,15},{1,0},{2,1},{3,2},{4,3},{5,4},{6,5},{7,6},{8,7},{9,8},{10,9... | collective-permute-start | bytes 1572872 | tf_op jit(solution)/shard_map/lon_neighbours/ppermute | solution.py:283
  2.0 1.7 %copy-start.8 = (s32[2,8]{1,0:T(2,128)S(1)}, s32[2,8]{1,0:T(2,128)}, u32[]{:S(2)}) copy-start(s32[2,8]{1,0:T(2,128)} %param.15) | copy-start | bytes 196
  3.7 26.9 %copy-start = (f32[32,32,128]{2,1,0:T(8,128)S(1)}, f32[32,32,128]{2,1,0:T(8,128)}, u32[]{:S(2)}) copy-start(f32[32,32,128]{2,1,0:T(8,128)} %tracer.1) | copy-start | bytes 1572868
  3.8 11.0 %copy-start.4 = (bf16[128,432]{1,0:T(8,128)(2,1)S(1)}, bf16[128,432]{1,0:T(8,128)(2,1)}, u32[]{:S(2)}) copy-start(bf16[128,432]{1,0:T(8,128)(2,1)} %constant.58.clone.1.refs_1_) | copy-start | bytes 331780 | tf_op jit(solution)/shard_map/polar_rows/cond
  3.8 19.9 %all-to-all-start = ((f32[16,4,8,128]{3,2,1,0:T(8,128)}), f32[16,4,8,128]{3,2,1,0:T(8,128)S(1)}, u32[]{:S(2)}, u32[]{:S(2)}) async-start(f32[16,4,8,128]{3,2,1,0:T(8,128)} %get-tuple-element.20), calls=%async_computation | async-start | bytes 524288 | tf_op jit(solution)/shard_map/polar_rows/cond/branch_1_fun/all_to_all | solution.py:308
  14.7 1.0 %copy-start.3 = (bf16[768,256]{1,0:T(8,128)(2,1)S(1)}, bf16[768,256]{1,0:T(8,128)(2,1)}, u32[]{:S(2)}) copy-start(bf16[768,256]{1,0:T(8,128)(2,1)} %constant.59.clone.1.refs_2_) | copy-start | bytes 1179652 | tf_op jit(solution)/shard_map/polar_rows/cond
  15.7 0.9 %copy-start.5 = (bf16[144,384]{1,0:T(8,128)(2,1)S(1)}, bf16[144,384]{1,0:T(8,128)(2,1)}, u32[]{:S(2)}) copy-start(bf16[144,384]{1,0:T(8,128)(2,1)} %constant.57.clone.1.refs_0_) | copy-start | bytes 331780 | tf_op jit(solution)/shard_map/polar_rows/cond
  16.6 0.9 %copy-start.6 = (f32[2,72,128]{2,1,0:T(8,128)S(1)}, f32[2,72,128]{2,1,0:T(8,128)}, u32[]{:S(2)}) copy-start(f32[2,72,128]{2,1,0:T(8,128)} %constant.60.clone.1.refs_3_) | copy-start | bytes 221188 | tf_op jit(solution)/shard_map/polar_rows/cond
  25.8 12.9 %all-to-all-start.1 = ((f32[16,2,8,128]{3,2,1,0:T(8,128)}), f32[16,2,8,128]{3,2,1,0:T(8,128)S(1)}, u32[]{:S(2)}, u32[]{:S(2)}) async-start(f32[16,2,8,128]{3,2,1,0:T(8,128)} %get-tuple-element.43), calls=%async_computation.1 | async-start | bytes 262144 | tf_op jit(solution)/shard_map/polar_rows/all_to_all | solution.py:337
  30.6 0.8 %copy-start.7 = (s32[32,1]{0,1:T(1,128)S(1)}, s32[32,1]{0,1:T(1,128)}, u32[]{:S(2)}) copy-start(s32[32,1]{0,1:T(1,128)} %param.12) | copy-start | bytes 388
  30.8 0.7 %collective-permute-start.2 = (f32[3,2,32,128]{3,2,1,0:T(8,128)S(1)}, f32[3,2,32,128]{3,2,1,0:T(8,128)S(1)}, u32[]{:S(2)}, u32[]{:S(2)}) collective-permute-start(f32[3,2,32,128]{3,2,1,0:T(8,128)S(1)} %borders.2), channel_id=1, source_target_pairs={{16,32},{17,33},{18,34},{19,35},{20,36},{21,37},{22,38},{23,39},{2... | collective-permute-start | bytes 294920 | tf_op jit(solution)/shard_map/borders/ppermute | solution.py:283
  31.5 1.5 %copy-start.1 = (s32[32,128]{1,0:T(8,128)S(1)}, s32[32,128]{1,0:T(8,128)}, u32[]{:S(2)}) copy-start(s32[32,128]{1,0:T(8,128)} %offset.3) | copy-start | bytes 49156
  31.5 1.5 %copy-start.2 = (f32[32,128]{1,0:T(8,128)S(1)}, f32[32,128]{1,0:T(8,128)}, u32[]{:S(2)}) copy-start(f32[32,128]{1,0:T(8,128)} %fraction.3) | copy-start | bytes 49156
  31.6 1.4 %collective-permute-start.3 = (f32[3,2,32,128]{3,2,1,0:T(8,128)S(1)}, f32[3,2,32,128]{3,2,1,0:T(8,128)S(1)}, u32[]{:S(2)}, u32[]{:S(2)}) collective-permute-start(f32[3,2,32,128]{3,2,1,0:T(8,128)S(1)} %borders.3), channel_id=1, source_target_pairs={{0,16},{1,17},{2,18},{3,19},{4,20},{5,21},{6,22},{7,23},{8,24},{9,... | collective-permute-start | bytes 294920 | tf_op jit(solution)/shard_map/borders/ppermute | solution.py:283

commit v6 on v5

--- a/solution.py
+++ b/solution.py
@@ -15,6 +15,8 @@
 HL = 2
 HALF = NBLK // 2 + 1
 PROWS = 8
+FIRST, FIRST_BACK = 5, 11
+SHIFT = (FIRST - FIRST_BACK) % (2048 // 128)
 F32 = jnp.float32
 BF16 = jnp.bfloat16
 
@@ -130,7 +132,7 @@
     count = NBLK * PROWS
     half = HALF * PROWS
     anchor = band[:, 2].reshape(count, BLK).astype(jnp.int32)
-    place = ((anchor >> 7) & 15) * PROWS + ((anchor >> 11) & 7)
+    place = (((anchor >> 7) - FIRST) & 15) * PROWS + ((anchor >> 11) & 7)
     lanes = lax.broadcasted_iota(jnp.int32, (count, BLK), 1)
     chosen = jnp.where(place == lanes, 1.0, 0.0).astype(BF16)
     own = jnp.concatenate([band[:, 0].reshape(count, BLK), band[:, 1].reshape(count, BLK)], 1)
@@ -166,7 +168,10 @@
     removed = dot(back[...], pieces(both, 0))
     for c in range(2):
         kept = limited[c] - removed[:, c * BLK : (c + 1) * BLK]
-        out[:, c] = kept.reshape(NBLK, PROWS, BLK)
+        kept = kept.reshape(NBLK, PROWS, BLK)
+        out[SHIFT:, c] = kept[: NBLK - SHIFT]
+        if SHIFT:
+            out[:SHIFT, c] = kept[NBLK - SHIFT :]
 
 
 def column_rows(columns, first):
@@ -228,24 +233,39 @@
         store_row(out, j, cubic_limited(values, cells, weights))
 
 
-def merge_kernel(rows_done, polar, out, sem):
+def merge_kernel(rows_done, polar, out, sems):
     lat = lax.axis_index("lat")
     last = lax.axis_size("lat") - 1
+    channels = out.shape[0]
+    split = SHIFT * (channels // NBLK)
 
     @pl.when((lat == 0) | (lat == last))
     def _():
-        first = pl.multiple_of(jnp.where(lat == 0, 0, out.shape[1] - PROWS), PROWS)
-        copy = pltpu.make_async_copy(polar, out.at[:, pl.ds(first, PROWS), :], sem)
-        copy.start()
-        copy.wait()
+        rows = pl.ds(pl.multiple_of(jnp.where(lat == 0, 0, out.shape[1] - PROWS), PROWS), PROWS)
+        copies = []
+        for n, (here, there, count) in enumerate(
+            ((split, 0, channels - split), (0, channels - split, split))
+        ):
+            if count:
+                part = out.at[pl.ds(there, count), rows, :]
+                copies.append(
+                    pltpu.make_async_copy(polar.at[pl.ds(here, count)], part, sems.at[n])
+                )
+        for copy in copies:
+            copy.start()
+        for copy in copies:
+            copy.wait()
+
+
+def around_circle(band, first):
+    return [band * NBLK + (b + first) % NBLK for b in range(NBLK)]
 
 
 def return_groups(lat_count):
     last = lat_count - 1
     planes = [b + half for b in range(NBLK // 2) for half in (0, NBLK // 2)]
     others = [a * NBLK + b for b in planes for a in range(1, last)]
-    ends = [[a * NBLK + b for b in range(NBLK)] for a in (0, last)]
-    return ends + [others[n : n + NBLK] for n in range(0, len(others), NBLK)]
+    return [around_circle(0, FIRST_BACK), around_circle(last, FIRST_BACK)] + [others[n : n + NBLK] for n in range(0, len(others), NBLK)]
 
 
 def body(tracer, source, offset, fraction, cutoffs):
@@ -305,7 +325,8 @@
         )(source.reshape(1, rows), tracer, offset, fraction)
 
     def filter_band():
-        band = lax.all_to_all(packed, "lon", 0, 0)
+        groups = [around_circle(a, FIRST) for a in range(lat_count)]
+        band = lax.all_to_all(packed, ("lat", "lon"), 0, 0, axis_index_groups=groups)
         tables = fourier_tables()
         damping = jax.ShapeDtypeStruct((HALF * PROWS, BLK), F32)
         held = [jax.ShapeDtypeStruct(table.shape, table.dtype) for table in tables]
@@ -369,7 +390,7 @@
             field,
             [anyplace, anyplace],
             anyplace,
-            [dma],
+            [dma((2,))],
             4,
             1_000_000,
             input_output_aliases={0: 0},

time: 39.7 us -> 39.6 us (level)
  the two profiles are of different devices: /device:TPU:32 before, /device:TPU:1 now
where the time goes in v6:
time: 39.6 us; the launch traced here: 39.2 us
  starting transfers between devices  27.7 us (70%)
  waiting for transfers between devices  5.62 us (14%)
  Pallas kernels  5.04 us (13%)
  local copies, waits for them, and re-layouts  0.69 us (2%)
    ppermute x4, starting transfers between devices, moved(): return lax.ppermute(values, ('lat', 'lon'), pairs)  20.4 us
    all_to_all x1, starting transfers between devices, body(): lax.all_to_all(filtered, ('lat', 'lon'), 0, 0, axis_index_groups=return_g...  7.3 us
    ppermute x4, waiting for transfers between devices, moved(): return lax.ppermute(values, ('lat', 'lon'), pairs)  5.61 us
    pallas_call x1, Pallas kernels, body(): call(rows_kernel, field, [smem] + [vmem] * 7, vmem, [pltpu.VMEM((4, rows,...  3.17 us
    pallas_call x1, Pallas kernels, body(): call(pack_kernel, jax.ShapeDtypeStruct((NBLK, 4, PROWS, BLK), F32), [anyp...  1.68 us
  transfers between devices with their start and end apart: 5, of which 3 were waited for; matrix products, arithmetic and copies ran while one was open for 2% of the time, Pallas kernels for 13%

profile of v6, /device:TPU:1, one launch (start us, length us, event | category | flops | bytes accessed | tf_op | source)
XLA Modules:
  0.0 39.2 jit_solution(5451014554657274907)
XLA Ops:
  0.0 2.5 %collective-permute-start.1 = (f32[32,32,128]{2,1,0:T(8,128)}, f32[32,32,128]{2,1,0:T(8,128)S(1)}, u32[]{:S(2)}, u32[]{:S(2)}) collective-permute-start(f32[32,32,128]{2,1,0:T(8,128)} %tracer.1), channel_id=1, source_target_pairs={{0,1},{1,2},{2,3},{3,4},{4,5},{5,6},{6,7},{7,8},{8,9},{9,10},{10,1... | collective-permute-start | bytes 1572872 | tf_op jit(solution)/shard_map/lon_neighbours/ppermute | solution.py:303
  2.5 5.0 %collective-permute-start = (f32[32,32,128]{2,1,0:T(8,128)}, f32[32,32,128]{2,1,0:T(8,128)S(1)}, u32[]{:S(2)}, u32[]{:S(2)}) collective-permute-start(f32[32,32,128]{2,1,0:T(8,128)} %tracer.1), channel_id=1, source_target_pairs={{0,15},{1,0},{2,1},{3,2},{4,3},{5,4},{6,5},{7,6},{8,7},{9,8},{10,9... | collective-permute-start | bytes 1572872 | tf_op jit(solution)/shard_map/lon_neighbours/ppermute | solution.py:303
  7.4 0.0 copy-start.8
  7.4 1.7 %pack_polar_band.1 = f32[16,4,8,128]{3,2,1,0:T(8,128)} custom-call(s32[1,32]{1,0:T(1,128)} %bitcast.9, f32[32,32,128]{2,1,0:T(8,128)} %tracer.1, s32[32,128]{1,0:T(8,128)} %offset.3, f32[32,128]{1,0:T(8,128)} %fraction.3), custom_call_target="tpu_custom_call" | custom-call | flops 1000000 | bytes 1048576 | tf_op jit(solution)/shard_map/pack_polar_band/pallas_call | solution.py:311
  9.1 0.0 copy-done.8
  9.1 0.0 copy-start
  9.1 0.7 %conditional.1 = (f32[16,2,8,128]{3,2,1,0:T(8,128)}) conditional(s32[]{:T(128)} %convert_element_type.3, () %tuple.11, (f32[16,4,8,128]{3,2,1,0:T(8,128)}, s32[2,8]{1,0:T(2,128)S(1)}, (), (), (), /*index=5*/()) %tuple.26), branch_computations={%region_0.0_spmd, %region_1.0_spmd} | conditional | flops 1400000000 | bytes 5636248 | solution.py:353
  9.1 0.7 %broadcast.155 = f32[16,2,8,128]{3,2,1,0:T(8,128)} broadcast(f32[]{:T(128)} %constant.46.clone), dimensions={} | broadcast | bytes 131076 | tf_op jit(solution)/shard_map/broadcast.1
  9.8 7.3 %all-to-all-start.1 = ((f32[16,2,8,128]{3,2,1,0:T(8,128)}), f32[16,2,8,128]{3,2,1,0:T(8,128)S(1)}, u32[]{:S(2)}, u32[]{:S(2)}) async-start(f32[16,2,8,128]{3,2,1,0:T(8,128)} %get-tuple-element.43), calls=%async_computation.1 | async-start | bytes 262144 | tf_op jit(solution)/shard_map/polar_rows/all_to_all | solution.py:358
  17.1 0.0 copy-start.7
  17.1 2.1 %collective-permute-done.1.west = f32[32,32,128]{2,1,0:T(8,128)S(1)} collective-permute-done((f32[32,32,128]{2,1,0:T(8,128)}, f32[32,32,128]{2,1,0:T(8,128)S(1)}, u32[]{:S(2)}, u32[]{:S(2)}) %collective-permute-start.1) | collective-permute-done | bytes 524320 | tf_op jit(solution)/shard_map/lon_neighbours/ppermute | solution.py:303
  19.3 0.0 collective-permute-done.east
  19.3 0.0 copy-done
  19.3 0.1 borders.2
  19.4 5.6 %collective-permute-start.2 = (f32[3,2,32,128]{3,2,1,0:T(8,128)S(1)}, f32[3,2,32,128]{3,2,1,0:T(8,128)S(1)}, u32[]{:S(2)}, u32[]{:S(2)}) collective-permute-start(f32[3,2,32,128]{3,2,1,0:T(8,128)S(1)} %borders.2), channel_id=1, source_target_pairs={{16,32},{17,33},{18,34},{19,35},{20,36},{21,37},{22,38},{23,39},{2... | collective-permute-start | bytes 294920 | tf_op jit(solution)/shard_map/borders/ppermute | solution.py:303
  25.0 0.0 copy-done.7
  25.1 0.0 copy-start.1
  25.1 0.0 copy-start.2
  25.1 2.5 %collective-permute-done.2.refs_0_.other = f32[3,2,32,128]{3,2,1,0:T(8,128)S(1)} collective-permute-done((f32[3,2,32,128]{3,2,1,0:T(8,128)S(1)}, f32[3,2,32,128]{3,2,1,0:T(8,128)S(1)}, u32[]{:S(2)}, u32[]{:S(2)}) %collective-permute-start.2) | collective-permute-done | bytes 98336 | tf_op jit(solution)/shard_map/borders/ppermute | solution.py:303
  27.6 0.1 borders.3
  27.7 7.3 %collective-permute-start.3 = (f32[3,2,32,128]{3,2,1,0:T(8,128)S(1)}, f32[3,2,32,128]{3,2,1,0:T(8,128)S(1)}, u32[]{:S(2)}, u32[]{:S(2)}) collective-permute-start(f32[3,2,32,128]{3,2,1,0:T(8,128)S(1)} %borders.3), channel_id=1, source_target_pairs={{0,16},{1,17},{2,18},{3,19},{4,20},{5,21},{6,22},{7,23},{8,24},{9,... | collective-permute-start | bytes 294920 | tf_op jit(solution)/shard_map/borders/ppermute | solution.py:303
  35.1 0.9 %collective-permute-done.3.pair = f32[3,2,32,128]{3,2,1,0:T(8,128)S(1)} collective-permute-done((f32[3,2,32,128]{3,2,1,0:T(8,128)S(1)}, f32[3,2,32,128]{3,2,1,0:T(8,128)S(1)}, u32[]{:S(2)}, u32[]{:S(2)}) %collective-permute-start.3) | collective-permute-done | bytes 98336 | tf_op jit(solution)/shard_map/borders/ppermute | solution.py:303
  36.0 0.0 copy-done.1
  36.0 0.0 copy-done.2
  36.0 3.2 %other_rows.1.rows_done = f32[32,32,128]{2,1,0:T(8,128)} custom-call(s32[2,32]{1,0:T(2,128)S(1)} %pad_add_fusion.place, s32[32,128]{1,0:T(8,128)S(1)} %copy-done.1, f32[32,128]{1,0:T(8,128)S(1)} %copy-done.2, f32[32,32,128]{2,1,0:T(8,128)S(1)} %collective-permute-done.east, f32[32,32,128]{2,1,0:T(8,128)S(1)} %copy-done, ...), custom_call_target="tpu_custom_call" | custom-call | flops 3000000000 | bytes 1048576 | tf_op jit(solution)/shard_map/other_rows/pallas_call | solution.py:377
  39.2 0.0 all-to-all-done.1
  (3 shorter events, 0.1 us)
Async XLA Ops:
  0.0 19.3 %collective-permute-start.1 = (f32[32,32,128]{2,1,0:T(8,128)}, f32[32,32,128]{2,1,0:T(8,128)S(1)}, u32[]{:S(2)}, u32[]{:S(2)}) collective-permute-start(f32[32,32,128]{2,1,0:T(8,128)} %tracer.1), channel_id=1, source_target_pairs={{0,1},{1,2},{2,3},{3,4},{4,5},{5,6},{6,7},{7,8},{8,9},{9,10},{10,1... | collective-permute-start | bytes 1572872 | tf_op jit(solution)/shard_map/lon_neighbours/ppermute | solution.py:303
  2.5 16.8 %collective-permute-start = (f32[32,32,128]{2,1,0:T(8,128)}, f32[32,32,128]{2,1,0:T(8,128)S(1)}, u32[]{:S(2)}, u32[]{:S(2)}) collective-permute-start(f32[32,32,128]{2,1,0:T(8,128)} %tracer.1), channel_id=1, source_target_pairs={{0,15},{1,0},{2,1},{3,2},{4,3},{5,4},{6,5},{7,6},{8,7},{9,8},{10,9... | collective-permute-start | bytes 1572872 | tf_op jit(solution)/shard_map/lon_neighbours/ppermute | solution.py:303
  7.4 1.7 %copy-start.8 = (s32[2,8]{1,0:T(2,128)S(1)}, s32[2,8]{1,0:T(2,128)}, u32[]{:S(2)}) copy-start(s32[2,8]{1,0:T(2,128)} %param.15) | copy-start | bytes 196
  9.1 10.2 %copy-start = (f32[32,32,128]{2,1,0:T(8,128)S(1)}, f32[32,32,128]{2,1,0:T(8,128)}, u32[]{:S(2)}) copy-start(f32[32,32,128]{2,1,0:T(8,128)} %tracer.1) | copy-start | bytes 1572868
  9.8 29.4 %all-to-all-start.1 = ((f32[16,2,8,128]{3,2,1,0:T(8,128)}), f32[16,2,8,128]{3,2,1,0:T(8,128)S(1)}, u32[]{:S(2)}, u32[]{:S(2)}) async-start(f32[16,2,8,128]{3,2,1,0:T(8,128)} %get-tuple-element.43), calls=%async_computation.1 | async-start | bytes 262144 | tf_op jit(solution)/shard_map/polar_rows/all_to_all | solution.py:358
  17.1 7.9 %copy-start.7 = (s32[32,1]{0,1:T(1,128)S(1)}, s32[32,1]{0,1:T(1,128)}, u32[]{:S(2)}) copy-start(s32[32,1]{0,1:T(1,128)} %param.12) | copy-start | bytes 388
  19.4 8.2 %collective-permute-start.2 = (f32[3,2,32,128]{3,2,1,0:T(8,128)S(1)}, f32[3,2,32,128]{3,2,1,0:T(8,128)S(1)}, u32[]{:S(2)}, u32[]{:S(2)}) collective-permute-start(f32[3,2,32,128]{3,2,1,0:T(8,128)S(1)} %borders.2), channel_id=1, source_target_pairs={{16,32},{17,33},{18,34},{19,35},{20,36},{21,37},{22,38},{23,39},{2... | collective-permute-start | bytes 294920 | tf_op jit(solution)/shard_map/borders/ppermute | solution.py:303
  25.1 10.9 %copy-start.1 = (s32[32,128]{1,0:T(8,128)S(1)}, s32[32,128]{1,0:T(8,128)}, u32[]{:S(2)}) copy-start(s32[32,128]{1,0:T(8,128)} %offset.3) | copy-start | bytes 49156
  25.1 10.9 %copy-start.2 = (f32[32,128]{1,0:T(8,128)S(1)}, f32[32,128]{1,0:T(8,128)}, u32[]{:S(2)}) copy-start(f32[32,128]{1,0:T(8,128)} %fraction.3) | copy-start | bytes 49156
  27.7 8.3 %collective-permute-start.3 = (f32[3,2,32,128]{3,2,1,0:T(8,128)S(1)}, f32[3,2,32,128]{3,2,1,0:T(8,128)S(1)}, u32[]{:S(2)}, u32[]{:S(2)}) collective-permute-start(f32[3,2,32,128]{3,2,1,0:T(8,128)S(1)} %borders.3), channel_id=1, source_target_pairs={{0,16},{1,17},{2,18},{3,19},{4,20},{5,21},{6,22},{7,23},{8,24},{9,... | collective-permute-start | bytes 294920 | tf_op jit(solution)/shard_map/borders/ppermute | solution.py:303

commit v7 on v6

--- a/solution.py
+++ b/solution.py
@@ -18,15 +18,16 @@
 FIRST, FIRST_BACK = 5, 11
 SHIFT = (FIRST - FIRST_BACK) % (2048 // 128)
 F32 = jnp.float32
+SIXTH = 1.0 / 6.0
 BF16 = jnp.bfloat16
 
 
 def cubic_weights(position):
     return (
-        -position * (position - 1.0) * (position - 2.0) / 6.0,
-        (position + 1.0) * (position - 1.0) * (position - 2.0) / 2.0,
-        -(position + 1.0) * position * (position - 2.0) / 2.0,
-        (position + 1.0) * position * (position - 1.0) / 6.0,
+        -position * (position - 1.0) * (position - 2.0) * SIXTH,
+        (position + 1.0) * (position - 1.0) * (position - 2.0) * 0.5,
+        -(position + 1.0) * position * (position - 2.0) * 0.5,
+        (position + 1.0) * position * (position - 1.0) * SIXTH,
     )
 
 

time: 39.6 us -> 39.6 us (level)
  no operation moved by 1% of the time
where the time goes in v7:
time: 39.6 us; the launch traced here: 39.2 us
  starting transfers between devices  27.7 us (70%)
  waiting for transfers between devices  5.62 us (14%)
  Pallas kernels  5.04 us (13%)
  local copies, waits for them, and re-layouts  0.69 us (2%)
    ppermute x4, starting transfers between devices, moved(): return lax.ppermute(values, ('lat', 'lon'), pairs)  20.4 us
    all_to_all x1, starting transfers between devices, body(): lax.all_to_all(filtered, ('lat', 'lon'), 0, 0, axis_index_groups=return_g...  7.3 us
    ppermute x4, waiting for transfers between devices, moved(): return lax.ppermute(values, ('lat', 'lon'), pairs)  5.61 us
    pallas_call x1, Pallas kernels, body(): call(rows_kernel, field, [smem] + [vmem] * 7, vmem, [pltpu.VMEM((4, rows,...  3.17 us
    pallas_call x1, Pallas kernels, body(): call(pack_kernel, jax.ShapeDtypeStruct((NBLK, 4, PROWS, BLK), F32), [anyp...  1.68 us
  transfers between devices with their start and end apart: 5, of which 3 were waited for; matrix products, arithmetic and copies ran while one was open for 2% of the time, Pallas kernels for 13%

profile of v7, /device:TPU:1, one launch (start us, length us, event | category | flops | bytes accessed | tf_op | source)
XLA Modules:
  0.0 39.2 jit_solution(5451014554657274907)
XLA Ops:
  0.0 2.5 %collective-permute-start.1 = (f32[32,32,128]{2,1,0:T(8,128)}, f32[32,32,128]{2,1,0:T(8,128)S(1)}, u32[]{:S(2)}, u32[]{:S(2)}) collective-permute-start(f32[32,32,128]{2,1,0:T(8,128)} %tracer.1), channel_id=1, source_target_pairs={{0,1},{1,2},{2,3},{3,4},{4,5},{5,6},{6,7},{7,8},{8,9},{9,10},{10,1... | collective-permute-start | bytes 1572872 | tf_op jit(solution)/shard_map/lon_neighbours/ppermute | solution.py:304
  2.5 5.0 %collective-permute-start = (f32[32,32,128]{2,1,0:T(8,128)}, f32[32,32,128]{2,1,0:T(8,128)S(1)}, u32[]{:S(2)}, u32[]{:S(2)}) collective-permute-start(f32[32,32,128]{2,1,0:T(8,128)} %tracer.1), channel_id=1, source_target_pairs={{0,15},{1,0},{2,1},{3,2},{4,3},{5,4},{6,5},{7,6},{8,7},{9,8},{10,9... | collective-permute-start | bytes 1572872 | tf_op jit(solution)/shard_map/lon_neighbours/ppermute | solution.py:304
  7.4 0.0 copy-start.8
  7.4 1.7 %pack_polar_band.1 = f32[16,4,8,128]{3,2,1,0:T(8,128)} custom-call(s32[1,32]{1,0:T(1,128)} %bitcast.9, f32[32,32,128]{2,1,0:T(8,128)} %tracer.1, s32[32,128]{1,0:T(8,128)} %offset.3, f32[32,128]{1,0:T(8,128)} %fraction.3), custom_call_target="tpu_custom_call" | custom-call | flops 1000000 | bytes 1048576 | tf_op jit(solution)/shard_map/pack_polar_band/pallas_call | solution.py:312
  9.1 0.0 copy-done.8
  9.1 0.0 copy-start
  9.1 0.7 %conditional.1 = (f32[16,2,8,128]{3,2,1,0:T(8,128)}) conditional(s32[]{:T(128)} %convert_element_type.3, () %tuple.11, (f32[16,4,8,128]{3,2,1,0:T(8,128)}, s32[2,8]{1,0:T(2,128)S(1)}, (), (), (), /*index=5*/()) %tuple.26), branch_computations={%region_0.0_spmd, %region_1.0_spmd} | conditional | flops 1400000000 | bytes 5636248 | solution.py:354
  9.1 0.7 %broadcast.155 = f32[16,2,8,128]{3,2,1,0:T(8,128)} broadcast(f32[]{:T(128)} %constant.46.clone), dimensions={} | broadcast | bytes 131076 | tf_op jit(solution)/shard_map/broadcast.1
  9.8 7.3 %all-to-all-start.1 = ((f32[16,2,8,128]{3,2,1,0:T(8,128)}), f32[16,2,8,128]{3,2,1,0:T(8,128)S(1)}, u32[]{:S(2)}, u32[]{:S(2)}) async-start(f32[16,2,8,128]{3,2,1,0:T(8,128)} %get-tuple-element.43), calls=%async_computation.1 | async-start | bytes 262144 | tf_op jit(solution)/shard_map/polar_rows/all_to_all | solution.py:359
  17.1 0.0 copy-start.7
  17.1 2.1 %collective-permute-done.1.west = f32[32,32,128]{2,1,0:T(8,128)S(1)} collective-permute-done((f32[32,32,128]{2,1,0:T(8,128)}, f32[32,32,128]{2,1,0:T(8,128)S(1)}, u32[]{:S(2)}, u32[]{:S(2)}) %collective-permute-start.1) | collective-permute-done | bytes 524320 | tf_op jit(solution)/shard_map/lon_neighbours/ppermute | solution.py:304
  19.3 0.0 collective-permute-done.east
  19.3 0.0 copy-done
  19.3 0.1 borders.2
  19.4 5.6 %collective-permute-start.2 = (f32[3,2,32,128]{3,2,1,0:T(8,128)S(1)}, f32[3,2,32,128]{3,2,1,0:T(8,128)S(1)}, u32[]{:S(2)}, u32[]{:S(2)}) collective-permute-start(f32[3,2,32,128]{3,2,1,0:T(8,128)S(1)} %borders.2), channel_id=1, source_target_pairs={{16,32},{17,33},{18,34},{19,35},{20,36},{21,37},{22,38},{23,39},{2... | collective-permute-start | bytes 294920 | tf_op jit(solution)/shard_map/borders/ppermute | solution.py:304
  25.0 0.0 copy-done.7
  25.1 0.0 copy-start.1
  25.1 0.0 copy-start.2
  25.1 2.5 %collective-permute-done.2.refs_0_.other = f32[3,2,32,128]{3,2,1,0:T(8,128)S(1)} collective-permute-done((f32[3,2,32,128]{3,2,1,0:T(8,128)S(1)}, f32[3,2,32,128]{3,2,1,0:T(8,128)S(1)}, u32[]{:S(2)}, u32[]{:S(2)}) %collective-permute-start.2) | collective-permute-done | bytes 98336 | tf_op jit(solution)/shard_map/borders/ppermute | solution.py:304
  27.6 0.1 borders.3
  27.7 7.3 %collective-permute-start.3 = (f32[3,2,32,128]{3,2,1,0:T(8,128)S(1)}, f32[3,2,32,128]{3,2,1,0:T(8,128)S(1)}, u32[]{:S(2)}, u32[]{:S(2)}) collective-permute-start(f32[3,2,32,128]{3,2,1,0:T(8,128)S(1)} %borders.3), channel_id=1, source_target_pairs={{0,16},{1,17},{2,18},{3,19},{4,20},{5,21},{6,22},{7,23},{8,24},{9,... | collective-permute-start | bytes 294920 | tf_op jit(solution)/shard_map/borders/ppermute | solution.py:304
  35.1 0.9 %collective-permute-done.3.pair = f32[3,2,32,128]{3,2,1,0:T(8,128)S(1)} collective-permute-done((f32[3,2,32,128]{3,2,1,0:T(8,128)S(1)}, f32[3,2,32,128]{3,2,1,0:T(8,128)S(1)}, u32[]{:S(2)}, u32[]{:S(2)}) %collective-permute-start.3) | collective-permute-done | bytes 98336 | tf_op jit(solution)/shard_map/borders/ppermute | solution.py:304
  36.0 0.0 copy-done.1
  36.0 0.0 copy-done.2
  36.0 3.2 %other_rows.1.rows_done = f32[32,32,128]{2,1,0:T(8,128)} custom-call(s32[2,32]{1,0:T(2,128)S(1)} %pad_add_fusion.place, s32[32,128]{1,0:T(8,128)S(1)} %copy-done.1, f32[32,128]{1,0:T(8,128)S(1)} %copy-done.2, f32[32,32,128]{2,1,0:T(8,128)S(1)} %collective-permute-done.east, f32[32,32,128]{2,1,0:T(8,128)S(1)} %copy-done, ...), custom_call_target="tpu_custom_call" | custom-call | flops 3000000000 | bytes 1048576 | tf_op jit(solution)/shard_map/other_rows/pallas_call | solution.py:378
  39.2 0.0 all-to-all-done.1
  (3 shorter events, 0.1 us)
Async XLA Ops:
  0.0 19.3 %collective-permute-start.1 = (f32[32,32,128]{2,1,0:T(8,128)}, f32[32,32,128]{2,1,0:T(8,128)S(1)}, u32[]{:S(2)}, u32[]{:S(2)}) collective-permute-start(f32[32,32,128]{2,1,0:T(8,128)} %tracer.1), channel_id=1, source_target_pairs={{0,1},{1,2},{2,3},{3,4},{4,5},{5,6},{6,7},{7,8},{8,9},{9,10},{10,1... | collective-permute-start | bytes 1572872 | tf_op jit(solution)/shard_map/lon_neighbours/ppermute | solution.py:304
  2.5 16.8 %collective-permute-start = (f32[32,32,128]{2,1,0:T(8,128)}, f32[32,32,128]{2,1,0:T(8,128)S(1)}, u32[]{:S(2)}, u32[]{:S(2)}) collective-permute-start(f32[32,32,128]{2,1,0:T(8,128)} %tracer.1), channel_id=1, source_target_pairs={{0,15},{1,0},{2,1},{3,2},{4,3},{5,4},{6,5},{7,6},{8,7},{9,8},{10,9... | collective-permute-start | bytes 1572872 | tf_op jit(solution)/shard_map/lon_neighbours/ppermute | solution.py:304
  7.4 1.7 %copy-start.8 = (s32[2,8]{1,0:T(2,128)S(1)}, s32[2,8]{1,0:T(2,128)}, u32[]{:S(2)}) copy-start(s32[2,8]{1,0:T(2,128)} %param.15) | copy-start | bytes 196
  9.1 10.2 %copy-start = (f32[32,32,128]{2,1,0:T(8,128)S(1)}, f32[32,32,128]{2,1,0:T(8,128)}, u32[]{:S(2)}) copy-start(f32[32,32,128]{2,1,0:T(8,128)} %tracer.1) | copy-start | bytes 1572868
  9.8 29.4 %all-to-all-start.1 = ((f32[16,2,8,128]{3,2,1,0:T(8,128)}), f32[16,2,8,128]{3,2,1,0:T(8,128)S(1)}, u32[]{:S(2)}, u32[]{:S(2)}) async-start(f32[16,2,8,128]{3,2,1,0:T(8,128)} %get-tuple-element.43), calls=%async_computation.1 | async-start | bytes 262144 | tf_op jit(solution)/shard_map/polar_rows/all_to_all | solution.py:359
  17.1 7.9 %copy-start.7 = (s32[32,1]{0,1:T(1,128)S(1)}, s32[32,1]{0,1:T(1,128)}, u32[]{:S(2)}) copy-start(s32[32,1]{0,1:T(1,128)} %param.12) | copy-start | bytes 388
  19.4 8.2 %collective-permute-start.2 = (f32[3,2,32,128]{3,2,1,0:T(8,128)S(1)}, f32[3,2,32,128]{3,2,1,0:T(8,128)S(1)}, u32[]{:S(2)}, u32[]{:S(2)}) collective-permute-start(f32[3,2,32,128]{3,2,1,0:T(8,128)S(1)} %borders.2), channel_id=1, source_target_pairs={{16,32},{17,33},{18,34},{19,35},{20,36},{21,37},{22,38},{23,39},{2... | collective-permute-start | bytes 294920 | tf_op jit(solution)/shard_map/borders/ppermute | solution.py:304
  25.1 10.9 %copy-start.1 = (s32[32,128]{1,0:T(8,128)S(1)}, s32[32,128]{1,0:T(8,128)}, u32[]{:S(2)}) copy-start(s32[32,128]{1,0:T(8,128)} %offset.3) | copy-start | bytes 49156
  25.1 10.9 %copy-start.2 = (f32[32,128]{1,0:T(8,128)S(1)}, f32[32,128]{1,0:T(8,128)}, u32[]{:S(2)}) copy-start(f32[32,128]{1,0:T(8,128)} %fraction.3) | copy-start | bytes 49156
  27.7 8.3 %collective-permute-start.3 = (f32[3,2,32,128]{3,2,1,0:T(8,128)S(1)}, f32[3,2,32,128]{3,2,1,0:T(8,128)S(1)}, u32[]{:S(2)}, u32[]{:S(2)}) collective-permute-start(f32[3,2,32,128]{3,2,1,0:T(8,128)S(1)} %borders.3), channel_id=1, source_target_pairs={{0,16},{1,17},{2,18},{3,19},{4,20},{5,21},{6,22},{7,23},{8,24},{9,... | collective-permute-start | bytes 294920 | tf_op jit(solution)/shard_map/borders/ppermute | solution.py:304
